TPU v7x, 32 devices: a whole 2x2x4 slice. The times are simulated.
32 devices in a mesh: row: 4 (over z), col: 4 (over y, x), ch: 2 (over core).
Axes of the slice: x: 2, y: 2, z: 4, core: 2. Of those that a mesh axis runs over, the one named last changes fastest.
Arguments:
- field: float32 [32, 512, 2048], P(None, 'row', 'col'), may hold values from -6 to 6
- spec_weight: float32 [2, 32, 32, 512], replicated, may hold values from -0.75 to 0.75
- point_weight: float32 [32, 32], replicated, may hold values from -1 to 1
- bias: float32 [32], P('ch'), may hold values from -1 to 1
- kept_modes: int32 [32], replicated, may hold values from 8 to 16, as said below
- residual: float32 [32, 16384], P('ch', ('row', 'col')), may hold values from -6 to 6
- trace_dest: int32 [16384, 1], P(('row', 'col')), may hold values from 0 to 15; in each aligned block of 1024 rows (0 to 1023, 1024 to 2047, ...) at most 128 rows name the same one
- trace_cell: int32 [16384], P(('row', 'col')), may hold values from 0 to 65535
Outputs:
- grad_field: float32 [32, 512, 2048], P('ch', 'row', 'col')
- grad_spec: float32 [2, 32, 32, 512], P(None, None, 'ch')
- grad_point: float32 [32, 32], P(None, 'ch')
- grad_bias: float32 [32], P('ch')
Inputs may be any that keep to these rules, and one draw needn't show every extreme that they name: `trace_dest`: of the 1024 points of one device, at most 128 go to one tile. `kept_modes`: some channel keeps 16 and some keeps 16 // 2.
All inputs are finite; a program needn't handle non-finite values.
Results may differ from a plain program's by a relative error of at most 0.00012.
Values sent between devices are 32-bit elements; how exact they have to be, the bound alone decides.
A program may use at most 192 MiB of HBM per device.

v0:
```python
import functools
import math

import jax
import jax.numpy as jnp
from jax import lax
from jax.experimental import pallas as pl
from jax.experimental.pallas import tpu as pltpu
from jax.sharding import PartitionSpec as P

M = 16
A = 2 * M
MODES = A * M
RB = 8
F32 = jnp.float32
BF16 = jnp.bfloat16
FULL_TURN = 6.283185307179586
NN = (((1,), (0,)), ((), ()))
NT = (((1,), (1,)), ((), ()))
MIB = 1 << 20


def row_table(start_at, extent, period):
    frequency = jnp.arange(A, dtype=jnp.int32)
    frequency = jnp.where(frequency < M, frequency, frequency - A)
    places = start_at + jnp.arange(extent, dtype=jnp.int32)
    phases = frequency[:, None] * places[None, :] % period
    angles = phases.astype(F32) * (FULL_TURN / period)
    return jnp.concatenate((jnp.cos(angles), jnp.sin(angles)), axis=0)


def col_table(start_at, extent, period):
    frequency = jnp.arange(M, dtype=jnp.int32)
    places = start_at + jnp.arange(extent, dtype=jnp.int32)
    phases = frequency[:, None] * places[None, :] % period
    angles = phases.astype(F32) * (FULL_TURN / period)
    return jnp.concatenate((jnp.cos(angles), jnp.sin(angles)), axis=0)


def mode_mask(kept_modes):
    indices = jnp.arange(MODES, dtype=jnp.int32)
    row_mode = indices // M
    col_mode = indices % M
    row_rank = jnp.where(row_mode < M, row_mode, 2 * M - 1 - row_mode)
    allowed = (row_rank[None, :] < kept_modes[:, None]) & (col_mode[None, :] < kept_modes[:, None])
    return allowed.astype(F32)


def split2(x):
    hi = x.astype(BF16)
    return hi, (x - hi.astype(F32)).astype(BF16)


def mm(a, b, dims=NN):
    return lax.dot_general(a, b, dims, preferred_element_type=F32)


def dot3(a, b, dims=NN):
    return mm(a[0], b[0], dims) + (mm(a[0], b[1], dims) + mm(a[1], b[0], dims))


def stacked(x, axis):
    hi, low = split2(x)
    return jnp.concatenate((hi.astype(F32), low.astype(F32)), axis=axis).astype(BF16)


def dot_tall(a_stack, b):
    count = a_stack.shape[0] // 2
    hi, low = split2(b)
    both = mm(a_stack, hi)
    return both[:count] + both[count:] + mm(a_stack[:count], low)


def deep_left(x):
    hi = x.astype(BF16).astype(F32)
    return jnp.concatenate((hi, x - hi, hi), axis=1)


def deep_right(x):
    hi = x.astype(BF16).astype(F32)
    return jnp.concatenate((hi, hi, x - hi), axis=0).astype(BF16)


def pack(dest, vals, out_ref, tiles, cap):
    n = dest.shape[0]
    wide = max(tiles, 128)
    named = dest == lax.broadcasted_iota(jnp.int32, (n, wide), 1)
    one_hot = named.astype(F32).astype(BF16)
    before = (
        lax.broadcasted_iota(jnp.int32, (n, n), 1) < lax.broadcasted_iota(jnp.int32, (n, n), 0)
    )
    earlier = mm(before.astype(F32).astype(BF16), one_hot)
    rank = jnp.sum(jnp.where(named, earlier, 0.0), axis=1, keepdims=True)
    position = dest * cap + rank.astype(jnp.int32)
    rows = vals.shape[0]
    hi = vals.astype(BF16)
    left = vals - hi.astype(F32)
    mid = left.astype(BF16)
    low = (left - mid.astype(F32)).astype(BF16)
    parts = jnp.concatenate((hi.astype(F32), mid.astype(F32), low.astype(F32)), axis=0).astype(BF16)
    step = 512
    for first in range(0, tiles * cap, step):
        at = lax.broadcasted_iota(jnp.int32, (n, step), 1) + first
        place = (position == at).astype(F32).astype(BF16)
        got = mm(parts, place)
        got = got[:rows] + got[rows : 2 * rows] + got[2 * rows : 3 * rows]
        for at in range(0, step, cap):
            out_ref[(first + at) // cap] = got[:, at : at + cap]


def mode_lines(rows, tall, scale):
    side = tall.shape[1] // 2
    both = mm(stacked(rows, 0), stacked(tall, 1))
    grid = both[: 2 * A, : 2 * side] + both[2 * A :, : 2 * side] + both[: 2 * A, 2 * side :]
    re = (grid[:A, :side] - grid[A:, side:]) * scale
    im = (grid[A:, :side] + grid[:A, side:]) * (-scale)
    return [part[:, at : at + 128] for part in (re, im) for at in range(0, side, 128)]


def exact(a, b):
    return lax.dot_general(
        a, b, NN, precision=lax.Precision.HIGHEST, preferred_element_type=F32
    )


def iota(shape, axis):
    return lax.broadcasted_iota(jnp.int32, shape, axis)


def spread_rows(weights):
    a, b = weights.shape
    left = (iota((a * RB, a), 0) // RB == iota((a * RB, a), 1)).astype(F32)
    right = (iota((b, b * RB), 1) // RB == iota((b, b * RB), 0)).astype(F32)
    shape = (a * RB, b * RB)
    same = iota(shape, 0) % RB == iota(shape, 1) % RB
    return jnp.where(same, exact(exact(left, weights), right), 0.0)


def slope_kernel(
    n_row, n_col, scale, field_ref, grid_ref, tall_rows_ref, wide_cols_ref, tall_cols_ref,
    rows_ref, point_ref, bias_ref, got_ref,
    slope_ref, other_ref, out_ref,
    half_ref, hot_ref, v_ref, tall_ref, acc_ref, kron2_ref, wide2_ref, cols2_ref, rowid_ref,
    made_ref, swap_send, swap_recv, x_ref, landed, total, gathered, send1, recv1, send2, recv2,
):
    step = pl.program_id(0)
    n = n_row * n_col
    channels, block, width = slope_ref.shape
    steps = made_ref.shape[0]
    rows = channels * RB
    points = got_ref.shape[1]
    inputs = field_ref.shape[0]

    def swap(i):
        return pltpu.make_async_remote_copy(
            src_ref=made_ref.at[i],
            dst_ref=other_ref.at[:, pl.ds(i * block, block), :],
            send_sem=swap_send.at[i],
            recv_sem=swap_recv.at[i],
            device_id=device_at(n_row, n_col, 0, 1),
            device_id_type=MESH,
        )

    @pl.when(step == 0)
    def _():
        greet_all(n_row, n_col)
        tall_rows = deep_left(tall_rows_ref[...]).astype(BF16)
        for o in range(channels):
            half_ref[o] = deep_left(mm(tall_rows, deep_right(grid_ref[o])))
        vals = got_ref[:channels, :]
        hi = vals.astype(BF16).astype(F32)
        both = jnp.concatenate((hi, vals - hi), axis=0)
        both = jnp.broadcast_to(both[:, None, :], (2 * channels, RB, points))
        v_ref[...] = both.reshape(2 * rows, points).astype(BF16)
        cell = got_ref[channels : channels + 1, :].astype(jnp.int32) - 1
        rowid_ref[...] = jnp.where(cell < 0, -1, cell // width)
        colid = jnp.where(cell < 0, -1, cell % width).astype(F32)
        for first in range(0, points, 128):
            ids = jnp.broadcast_to(colid[:, first : first + 128], (128, 128)).T
            for at in range(0, width, 128):
                hot = ids == (iota((128, 128), 1) + at).astype(F32)
                hot_ref[first : first + 128, at : at + 128] = hot.astype(F32).astype(BF16)
        acc_ref[...] = jnp.zeros_like(acc_ref)
        kron2_ref[...] = stacked(spread_rows(point_ref[...]), 0)
        wide2_ref[...] = deep_right(wide_cols_ref[...])
        cols2_ref[...] = stacked(tall_cols_ref[...], 1)

    subs = block // RB
    picked = []
    for u in range(subs):
        first = step * block + u * RB
        here = rowid_ref[...] == first + lax.broadcasted_iota(jnp.int32, (RB, points), 0)
        here = here.astype(F32)
        here = jnp.concatenate((here, here), axis=0).astype(BF16)
        here = jnp.broadcast_to(here[None], (rows // RB, 2 * RB, points)).reshape(2 * rows, points)
        picked.append(v_ref[...] * here)
    cots = mm(jnp.concatenate(picked, axis=0), hot_ref[...])
    k = math.sqrt(2.0 / math.pi)
    fields, slopes = [], []
    for u in range(subs):
        first = pl.multiple_of(step * block + u * RB, RB)
        hi, low = split2(field_ref[:, u * RB : (u + 1) * RB, :].reshape(inputs * RB, width))
        half = half_ref[:, pl.ds(first, RB), :].reshape(rows, 6 * M).astype(BF16)
        both = mm(kron2_ref[...], hi)
        pre = (
            mm(half, wide2_ref[...])
            + (both[:rows] + both[rows:] + mm(kron2_ref[:rows, :], low))
            + bias_ref[...]
        )
        cot = cots[2 * rows * u : 2 * rows * u + rows] + cots[2 * rows * u + rows : 2 * rows * (u + 1)]
        square = pre * pre
        t = jnp.tanh(k * pre * (1.0 + 0.044715 * square))
        rate = 0.5 * (1.0 + t) + 0.5 * k * pre * (1.0 - t * t) * (1.0 + 3 * 0.044715 * square)
        slope = cot * rate
        slope_ref[:, u * RB : (u + 1) * RB, :] = slope.reshape(channels, RB, width)
        made_ref[step, :, u * RB : (u + 1) * RB, :] = slope.reshape(channels, RB, width)
        parts = stacked(slope, 0)
        got = mm(parts, cols2_ref[...])
        tall = got[:rows, : 2 * M] + got[:rows, 2 * M :] + got[rows:, : 2 * M]
        for o in range(channels):
            for part in range(2):
                at = (part * channels + o) * M
                tall_ref[pl.ds(first, RB), at : at + M] = tall[
                    o * RB : (o + 1) * RB, part * M : (part + 1) * M
                ]
        fields.append(jnp.concatenate((hi, low), axis=0))
        slopes.append(parts)
    acc_ref[...] += mm(jnp.concatenate(fields, axis=1), jnp.concatenate(slopes, axis=1), NT)

    @pl.when(step == 0)
    def _():
        pl.semaphore_wait(pltpu.get_barrier_semaphore(), 2 * n - 1)

    swap(step).start()

    @pl.when(step == steps - 1)
    def _():
        lines = mode_lines(rows_ref[...], tall_ref[...], scale)
        total_point = acc_ref[: inputs * RB, :] + acc_ref[inputs * RB :, :]
        total_point = total_point[:, :rows] + total_point[:, rows:]
        same = iota(total_point.shape, 0) % RB == iota(total_point.shape, 1) % RB
        kept = jnp.sum(jnp.where(same, total_point, 0.0).reshape(inputs, RB, rows), axis=1)
        each = 128 // channels
        group = (iota((rows, 128), 0) // RB == iota((rows, 128), 1) % channels).astype(F32)
        wide = exact(kept, group)
        own = iota(wide.shape, 1) // channels == iota(wide.shape, 0) % each
        lines.append(jnp.sum(jnp.where(own, wide, 0.0).reshape(inputs // each, each, 128), axis=1))
        deep = x_ref.shape[1]
        count = sum(line.shape[0] for line in lines)
        lines.append(jnp.zeros((n * deep - count, 128), F32))
        lines = jnp.concatenate(lines, axis=0)
        for p in range(n):
            x_ref[p] = lines[p * deep : (p + 1) * deep]
        sum_all(n_row, n_col, x_ref, landed, total, gathered, send1, recv1, send2, recv2)
        out_ref[...] = gathered[...]

        def end(i, carry):
            swap(i).wait()
            return carry

        lax.fori_loop(0, steps, end, 0)


def whole(shape):
    return pl.BlockSpec(shape, lambda i: (0,) * len(shape))


def slope_pass(
    field, grid, wide_cols, cols_t, rows, rows_t, point, bias, got, scale, n_row, n_col
):
    n = n_row * n_col
    inputs, height, width = field.shape
    channels = grid.shape[0]
    points = got.shape[1]
    lanes = channels * RB
    block = 2 * RB
    steps = height // block
    mode_count = channels * 2 * MODES // 128
    deep = -(-(mode_count + inputs * channels // 128) // n)
    args = (field, grid, rows_t, wide_cols, cols_t, rows, point, bias, got)
    slope, other, out = pl.pallas_call(
        functools.partial(slope_kernel, n_row, n_col, scale),
        grid=(steps,),
        in_specs=[pl.BlockSpec((inputs, block, width), lambda i: (0, i, 0))]
        + [whole(arg.shape) for arg in args[1:]],
        out_specs=[
            pl.BlockSpec((channels, block, width), lambda i: (0, i, 0)),
            pl.BlockSpec(memory_space=pl.ANY),
            whole((2 * n, deep, 128)),
        ],
        out_shape=[
            jax.ShapeDtypeStruct((channels, height, width), F32),
            jax.ShapeDtypeStruct((channels, height, width), F32),
            jax.ShapeDtypeStruct((2 * n, deep, 128), F32),
        ],
        scratch_shapes=[
            pltpu.VMEM((channels, height, 6 * M), F32),
            pltpu.VMEM((points, width), BF16),
            pltpu.VMEM((2 * lanes, points), BF16),
            pltpu.VMEM((height, 2 * channels * M), F32),
            pltpu.VMEM((2 * inputs * RB, 2 * lanes), F32),
            pltpu.VMEM((2 * lanes, inputs * RB), BF16),
            pltpu.VMEM((6 * M, width), BF16),
            pltpu.VMEM((width, 4 * M), BF16),
            pltpu.VMEM((1, points), jnp.int32),
            pltpu.VMEM((steps, channels, block, width), F32),
            pltpu.SemaphoreType.DMA((steps,)),
            pltpu.SemaphoreType.DMA((steps,)),
            pltpu.VMEM((n, deep, 128), F32),
            pltpu.VMEM((n, deep, 128), F32),
            pltpu.VMEM((deep, 128), F32),
            pltpu.VMEM((2 * n, deep, 128), F32),
            pltpu.SemaphoreType.DMA((n,)),
            pltpu.SemaphoreType.DMA((n,)),
            pltpu.SemaphoreType.DMA((2 * n,)),
            pltpu.SemaphoreType.DMA((2 * n,)),
        ],
        compiler_params=pltpu.CompilerParams(
            collective_id=1, has_side_effects=True, vmem_limit_bytes=52 * MIB
        ),
    )(*args)
    out = out.reshape(2, n * deep, 128)
    return slope, other, unfold(out[:, :mode_count], channels), out[:, mode_count:]


def back_kernel(
    own_ref, other_ref, grid_ref, tall_rows_ref, wide_cols_ref, point_ref, out_ref,
    half_ref, kron2_ref, wide2_ref,
):
    step = pl.program_id(0)
    channels, block, width = out_ref.shape
    rows = channels * RB

    @pl.when(step == 0)
    def _():
        tall_rows = deep_left(tall_rows_ref[...]).astype(BF16)
        for c in range(channels):
            half_ref[c] = deep_left(mm(tall_rows, deep_right(grid_ref[c])))
        kron2_ref[...] = stacked(spread_rows(point_ref[...]), 0)
        wide2_ref[...] = deep_right(wide_cols_ref[...])

    for u in range(block // RB):
        at = slice(u * RB, (u + 1) * RB)
        first = pl.multiple_of(step * block + u * RB, RB)
        half = half_ref[:, pl.ds(first, RB), :].reshape(rows, 6 * M).astype(BF16)
        slope = jnp.concatenate(
            (own_ref[:, at, :].reshape(rows, width), other_ref[:, at, :].reshape(rows, width)),
            axis=0,
        )
        result = mm(half, wide2_ref[...]) + dot_tall(kron2_ref[...], slope)
        out_ref[:, at, :] = result.reshape(channels, RB, width)


def back_pass(own, other, grid, rows_t, wide_cols, point):
    channels, height, width = own.shape
    args = (own, other, grid, rows_t, wide_cols, point)
    block = pl.BlockSpec((channels, 4 * RB, width), lambda i: (0, i, 0))
    return pl.pallas_call(
        back_kernel,
        grid=(height // (4 * RB),),
        in_specs=[block, block] + [whole(arg.shape) for arg in args[2:]],
        out_specs=block,
        out_shape=jax.ShapeDtypeStruct((channels, height, width), F32),
        scratch_shapes=[
            pltpu.VMEM((channels, height, 6 * M), F32),
            pltpu.VMEM((2 * point.shape[0] * RB, point.shape[1] * RB), BF16),
            pltpu.VMEM((6 * M, width), BF16),
        ],
        compiler_params=pltpu.CompilerParams(vmem_limit_bytes=52 * MIB),
    )(*args)


MESH = pl.DeviceIdType.MESH


def greet_all(n_row, n_col):
    n = n_row * n_col
    barrier = pltpu.get_barrier_semaphore()

    def greet(i, carry):
        pl.semaphore_signal(
            barrier, inc=1, device_id=device_at(n_row, n_col, i // 2, i % 2), device_id_type=MESH
        )
        return carry

    lax.fori_loop(1, 2 * n, greet, 0)
    return barrier


def device_at(n_row, n_col, offset, flip):
    n = n_row * n_col
    at = lax.rem(lax.axis_index("row") * n_col + lax.axis_index("col") + offset, n)
    return (at // n_col, lax.rem(at, n_col), lax.rem(lax.axis_index("ch") + flip, 2))


def send_slices(n_row, n_col, x_ref, landed, send, recv):
    n = n_row * n_col
    me = lax.axis_index("row") * n_col + lax.axis_index("col")

    def copy(k):
        return pltpu.make_async_remote_copy(
            src_ref=x_ref.at[lax.rem(me + k, n)],
            dst_ref=landed.at[k],
            send_sem=send.at[k],
            recv_sem=recv.at[k],
            device_id=device_at(n_row, n_col, k, 0),
            device_id_type=MESH,
        )

    def start(k, carry):
        copy(k).start()
        return carry

    lax.fori_loop(1, n, start, 0)
    return copy


def sum_all(n_row, n_col, x_ref, landed, total, gathered, send1, recv1, send2, recv2):
    n = n_row * n_col
    ch = lax.axis_index("ch")
    me = lax.axis_index("row") * n_col + lax.axis_index("col")
    scatter = send_slices(n_row, n_col, x_ref, landed, send1, recv1)
    total[...] = x_ref[me]

    def take(k, carry):
        scatter(k).wait_recv()
        total[...] += landed[k]
        return carry

    lax.fori_loop(1, n, take, 0)
    gathered[ch * n + me] = total[...]

    def spread(i):
        return pltpu.make_async_remote_copy(
            src_ref=total,
            dst_ref=gathered.at[ch * n + me],
            send_sem=send2.at[i],
            recv_sem=recv2.at[i],
            device_id=device_at(n_row, n_col, i // 2, i % 2),
            device_id_type=MESH,
        )

    def start2(i, carry):
        spread(i).start()
        return carry

    lax.fori_loop(1, 2 * n, start2, 0)

    def end1(k, carry):
        scatter(k).wait_send()
        return carry

    lax.fori_loop(1, n, end1, 0)

    def end2(i, carry):
        spread(i).wait()
        return carry

    lax.fori_loop(1, 2 * n, end2, 0)


def front_kernel(
    n_row, n_col, own, scale, dest_ref, vals_ref, cols_ref, rows_ref, field_ref, got_ref, out_ref,
    held, held_sem, grouped, came, tall_ref, x_ref, landed, total, gathered,
    send0, recv0, send1, recv1, send2, recv2,
):
    n = n_row * n_col
    count, height, width = held.shape[1:]
    cap = grouped.shape[2]
    ch = lax.axis_index("ch")
    me = lax.axis_index("row") * n_col + lax.axis_index("col")
    loads = [
        pltpu.make_async_copy(
            field_ref.at[pl.ds(ch * own + i * count, count)], held.at[i], held_sem.at[i]
        )
        for i in range(own // count)
    ]
    for load in loads:
        load.start()
    barrier = greet_all(n_row, n_col)
    pack(dest_ref[...], vals_ref[...], grouped, n, cap)
    pl.semaphore_wait(barrier, 2 * n - 1)
    trade = send_slices(n_row, n_col, grouped, came, send0, recv0)
    came[0] = grouped[me]

    cols2 = stacked(cols_ref[...], 1)
    for i, load in enumerate(loads):
        load.wait()
        both = mm(stacked(held[i].reshape(count * height, width), 0), cols2)
        half = count * height
        tall = both[:half, : 2 * M] + both[:half, 2 * M :] + both[half:, : 2 * M]
        for c in range(count):
            at = (i * count + c) * M
            tall_ref[:, at : at + M] = tall[c * height : (c + 1) * height, :M]
            at = at + own * M
            tall_ref[:, at : at + M] = tall[c * height : (c + 1) * height, M:]
    lines = jnp.concatenate(mode_lines(rows_ref[...], tall_ref[...], scale), axis=0)
    deep = lines.shape[0] // n
    for p in range(n):
        x_ref[p] = lines[p * deep : (p + 1) * deep]
    sum_all(n_row, n_col, x_ref, landed, total, gathered, send1, recv1, send2, recv2)
    out_ref[...] = gathered[...]

    def end0(k, carry):
        trade(k).wait()
        return carry

    lax.fori_loop(1, n, end0, 0)
    for p in range(n):
        got_ref[:, p * cap : (p + 1) * cap] = came[p]


def front_pass(dest, vals, cols_t, rows, field, own, cap, scale, n_row, n_col):
    n = n_row * n_col
    _, height, width = field.shape
    count = 4
    deep = own * 2 * MODES // 128 // n
    kept = vals.shape[0]
    vmem = pl.BlockSpec(memory_space=pltpu.VMEM)
    got, out = pl.pallas_call(
        functools.partial(front_kernel, n_row, n_col, own, scale),
        out_shape=[
            jax.ShapeDtypeStruct((kept, n * cap), F32),
            jax.ShapeDtypeStruct((2 * n, deep, 128), F32),
        ],
        in_specs=[vmem, vmem, vmem, vmem, pl.BlockSpec(memory_space=pl.ANY)],
        out_specs=[vmem, vmem],
        scratch_shapes=[
            pltpu.VMEM((own // count, count, height, width), F32),
            pltpu.SemaphoreType.DMA((own // count,)),
            pltpu.VMEM((n, kept, cap), F32),
            pltpu.VMEM((n, kept, cap), F32),
            pltpu.VMEM((height, 2 * own * M), F32),
            pltpu.VMEM((n, deep, 128), F32),
            pltpu.VMEM((n, deep, 128), F32),
            pltpu.VMEM((deep, 128), F32),
            pltpu.VMEM((2 * n, deep, 128), F32),
        ]
        + [pltpu.SemaphoreType.DMA((n,))] * 4
        + [pltpu.SemaphoreType.DMA((2 * n,))] * 2,
        compiler_params=pltpu.CompilerParams(
            collective_id=0, has_side_effects=True, vmem_limit_bytes=52 * MIB
        ),
    )(dest, vals, cols_t, rows, field)
    return got, unfold(out.reshape(2, n * deep, 128), own)


def unfold(lines, own):
    wide = 128 // M
    lines = lines.reshape(2, 2, own // wide, A, wide, M).transpose(1, 0, 2, 4, 3, 5)
    return lines.reshape(2, 2 * own, MODES)


def mode_grid(re, im):
    count = re.shape[0]
    re = re.reshape(count, A, M)
    im = im.reshape(count, A, M)
    return jnp.concatenate(
        (jnp.concatenate((re, im), axis=2), jnp.concatenate((-im, re), axis=2)), axis=1
    )


def per_device(
    field, spec_weight, point_weight, bias, kept_modes, residual, trace_dest, trace_cell
):
    n_row = lax.axis_size("row")
    n_col = lax.axis_size("col")
    ch = lax.axis_index("ch")
    inputs, height, width = field.shape
    own = inputs // lax.axis_size("ch")
    first = ch * own
    points = trace_dest.shape[0]
    tiles = n_row * n_col
    points_all = points * tiles
    cap = max(2, 2 * points // tiles)
    forward_scale = 1.0 / math.sqrt(height * n_row * width * n_col)
    mix_scale = 1.0 / math.sqrt(MODES)

    rows = row_table(lax.axis_index("row") * height, height, height * n_row)
    cols = col_table(lax.axis_index("col") * width, width, width * n_col)
    rows_t = rows.T
    cols_t = cols.T
    wide_cols = jnp.concatenate((cols[:M], -cols[M:]), axis=0)

    vals = jnp.concatenate(
        (residual, (trace_cell + 1).astype(F32)[None, :], jnp.zeros((7, points), F32)), axis=0
    )
    got, spec = front_pass(
        trace_dest, vals, cols_t, rows, field, own, cap, forward_scale, n_row, n_col
    )
    spec_re, spec_im = spec[0], spec[1]

    allowed = mode_mask(kept_modes)
    own_allowed = lax.dynamic_slice_in_dim(allowed, first, own, 0)
    out_w = lax.dynamic_slice_in_dim(spec_weight, first, own, 2)
    mixed_re = own_allowed * jnp.sum(
        out_w[0] * spec_re[:, None, :] - out_w[1] * spec_im[:, None, :], axis=0
    )
    mixed_im = own_allowed * jnp.sum(
        out_w[0] * spec_im[:, None, :] + out_w[1] * spec_re[:, None, :], axis=0
    )
    out_point = lax.dynamic_slice_in_dim(point_weight, first, own, 1).T
    slope, other_slope, modes, point_sum = slope_pass(
        field, mode_grid(mixed_re * mix_scale, mixed_im * mix_scale), wide_cols, cols_t, rows,
        rows_t, out_point, jnp.repeat(bias, RB)[:, None], got, mix_scale, n_row, n_col,
    )
    modes_re, modes_im = modes[0], modes[1]
    own_modes = lax.dynamic_slice_in_dim(modes, first, own, 1)
    own_gre, own_gim = own_modes[0], own_modes[1]
    point_lines = inputs * own // 128
    mine = lax.dynamic_slice_in_dim(point_sum, ch, 1, 0)[0, :point_lines]
    norm_points = 1.0 / math.sqrt(points_all)
    grad_point = mine.reshape(inputs, own) * norm_points
    grad_bias = own_gre[:, 0] * (norm_points / mix_scale)

    grad_scale = math.sqrt(MODES / points_all)
    keep_re = own_allowed * own_gre * grad_scale
    keep_im = own_allowed * own_gim * grad_scale
    grad_spec = jnp.stack(
        (
            keep_re[None] * spec_re[:, None] + keep_im[None] * spec_im[:, None],
            keep_im[None] * spec_re[:, None] - keep_re[None] * spec_im[:, None],
        ),
        axis=0,
    )
    in_w = lax.dynamic_slice_in_dim(spec_weight, first, own, 1)
    all_re = allowed * modes_re * forward_scale
    all_im = allowed * modes_im * forward_scale
    adjoint_re = jnp.sum(in_w[0] * all_re[None] + in_w[1] * all_im[None], axis=1)
    adjoint_im = jnp.sum(in_w[0] * all_im[None] - in_w[1] * all_re[None], axis=1)
    own_point = lax.dynamic_slice_in_dim(point_weight, first, own, 0)
    back_point = jnp.concatenate(
        (
            lax.dynamic_slice_in_dim(own_point, first, own, 1),
            lax.dynamic_slice_in_dim(own_point, own - first, own, 1),
        ),
        axis=1,
    )
    grad_field = back_pass(
        slope, other_slope, mode_grid(adjoint_re, adjoint_im), rows_t, wide_cols, back_point
    )
    return (grad_field, grad_spec, grad_point, grad_bias)


def solution(mesh):
    return jax.shard_map(
        per_device,
        mesh=mesh,
        in_specs=(
            P(None, "row", "col"),
            P(),
            P(),
            P("ch"),
            P(),
            P("ch", ("row", "col")),
            P(("row", "col"), None),
            P(("row", "col")),
        ),
        out_specs=(P("ch", "row", "col"), P(None, None, "ch", None), P(None, "ch"), P("ch")),
        check_vma=False,
    )
```

profile of v0, /device:TPU:0, one launch (start us, length us, event | category | flops | bytes accessed | tf_op | source)
XLA Modules:
  0.0 85.2 jit_solution(2946179335884059717)
XLA Ops:
  0.7 0.1 pad.20.clone
  0.7 0.7 add_convert_fusion
  1.4 0.7 broadcast_in_dim.8
  2.2 0.1 fusion.11
  2.3 0.9 %fusion.27 = (f32[16,16]{1,0:T(8,128)S(1)}, f32[16,16]{1,0:T(8,128)S(1)}) fusion(f32[32,32]{1,0:T(8,128)} %param.10, s32[]{:T(128)S(6)} %select_n.73, s32[]{:T(128)S(6)} %select_n.75), kind=kLoop, calls=%fused_computation.76 | loop fusion | bytes 4104 | tf_op jit(solution)/shard_map/dynamic_slice | solution.py:634
  3.1 0.1 pad_maximum_fusion.4.point_ref
  3.2 0.7 compare_and_fusion
  3.9 0.8 constant_dynamic-slice_fusion.1
  4.7 0.1 copy.69
  4.8 0.1 copy.54
  4.9 0.1 broadcast_in_dim_reshape.4.bias_ref
  5.0 0.2 multiply_cosine_fusion
  5.2 0.1 fusion.28.tall_rows_ref
  5.3 0.1 pad_maximum_fusion.3
  5.4 0.1 copy.57.rows_ref
  5.5 0.9 %maximum_maximum_fusion.2.vals_ref = f32[24,1024]{1,0:T(8,128)S(1)} fusion(f32[1,1024]{1,0:T(1,128)S(1)} %bitcast.56, f32[16,1024]{1,0:T(8,128)} %param.13, f32[24]{0:T(128)S(1)} %pad.20.clone), kind=kLoop, calls=%fused_computation.13 | loop fusion | flops 49152 | bytes 168032 | tf_op jit(solution)/shard_map/concatenate | solution.py:585
  6.4 0.1 fusion.15
  6.6 0.1 copy.56.cols_ref.tall_cols_ref
  6.7 0.9 %copy.55.dest_ref = s32[1024,1]{1,0:T(8,128)S(1)} copy(s32[1024,1]{0,1:T(1,128)} %param.14) | data formatting | bytes 8192 | tf_op args[6]
  7.6 21.7 %shard_map.111 = (f32[24,2048]{1,0:T(8,128)S(1)}, f32[32,8,128]{2,1,0:T(8,128)S(1)}) custom-call(s32[1024,1]{1,0:T(8,128)S(1)} %copy.55.dest_ref, f32[24,1024]{1,0:T(8,128)S(1)} %maximum_maximum_fusion.2.vals_ref, f32[512,32]{1,0:T(8,128)S(1)} %copy.56.cols_ref.tall_cols_ref, f32[64,128]{1,0:T(8,128)S(1)} %copy.57.rows_ref, f32[32,128,512]{2,1,0:T(8,128)} %field_ref.3), custom_call_target="tpu_custom_call" | custom-call | tf_op jit(solution)/shard_map/pallas_call | solution.py:520
  29.4 0.3 reshape_reshape.3
  29.7 0.1 fusion.25
  29.8 0.1 copy.58
  29.9 0.3 mul.251
  30.1 0.1 copy.59
  30.2 0.3 mul.254
  30.5 1.9 %add_reduce_fusion.1 = (f32[16,512]{1,0:T(8,128)S(1)}, f32[16,512]{1,0:T(8,128)S(1)}) fusion(f32[2,32,32,512]{3,2,1,0:T(8,128)} %param.9, s32[]{:T(128)S(6)} %select_n.69, s32[]{:T(128)S(6)} %add.110, f32[32,512]{1,0:T(8,128)S(1)} %mul.254, f32[32,512]{1,0:T(8,128)S(1)} %mul.251), kind=kLoop, calls=%fused_computation.9 | loop fusion | flops 2080768 | bytes 2293768 | tf_op jit(solution)/shard_map/reduce_sum | solution.py:599
  32.5 0.1 reshape.214
  32.6 0.1 reshape.213
  32.8 0.2 maximum_maximum_fusion.grid_ref
  33.0 35.3 %shard_map.112 = (f32[16,128,512]{2,1,0:T(8,128)}, f32[16,128,512]{2,1,0:T(8,128)}, f32[32,9,128]{2,1,0:T(8,128)S(1)}) custom-call(f32[32,128,512]{2,1,0:T(8,128)} %field_ref.3, f32[16,64,32]{2,1,0:T(8,128)S(1)} %maximum_maximum_fusion.grid_ref, f32[128,64]{1,0:T(8,128)S(1)} %fusion.28.tall_rows_ref, f32[32,512]{1,0:T(8,128)S(1)} %get-tuple-element.40.wide_cols_ref, ...), custom_call_target="tpu_custom_call" | custom-call | tf_op jit(solution)/shard_map/pallas_call | solution.py:281
  68.2 0.0 copy-start
  68.3 0.1 copy.64
  68.4 0.1 mul.287
  68.5 0.7 copy.68
  69.2 0.4 reshape.216
  69.6 0.3 fusion.26
  69.9 0.2 copy.65
  70.2 0.3 squeeze.32
  70.4 0.2 copy.66
  70.7 0.3 squeeze.34
  70.9 0.0 copy-done
  70.9 0.1 select_multiply_fusion.1
  71.0 2.0 %subtract_reduce_fusion = (f32[16,512]{1,0:T(8,128)S(1)}, f32[16,512]{1,0:T(8,128)S(1)}) fusion(f32[2,32,32,512]{3,2,1,0:T(8,128)} %param.9, s32[]{:T(128)S(6)} %select_n.69, s32[]{:T(128)S(6)} %add.110, f32[32,512]{1,0:T(8,128)S(1)} %get-tuple-element.47, f32[32,512]{1,0:T(8,128)S(1)} %get-tuple-element.46), kind=kLoop, calls=%fused_computation.7 | loop fusion | flops 2080768 | bytes 2293768 | tf_op jit(solution)/shard_map/reduce_sum | solution.py:630
  73.0 0.1 reshape.218
  73.1 0.1 reshape.217
  73.3 0.2 maximum_maximum_fusion.1.grid_ref
  73.5 8.1 %shard_map.113 = f32[16,128,512]{2,1,0:T(8,128)} custom-call(f32[16,128,512]{2,1,0:T(8,128)} %get-tuple-element.11.own_ref, f32[16,128,512]{2,1,0:T(8,128)} %get-tuple-element.12.other_ref, f32[16,64,32]{2,1,0:T(8,128)S(1)} %maximum_maximum_fusion.1.grid_ref, f32[128,64]{1,0:T(8,128)S(1)} %fusion.28.tall_rows_ref, ...), custom_call_target="tpu_custom_call" | custom-call | tf_op jit(solution)/shard_map/pallas_call | solution.py:358
  81.6 0.4 copy.67
  82.0 0.6 reshape.219
  82.7 0.6 fusion.16
  83.3 0.3 multiply_add_fusion
  83.6 1.6 %pad_maximum_fusion = f32[2,32,16,512]{3,2,1,0:T(8,128)} fusion(f32[1,32,16,512]{3,2,1,0:T(8,128)S(1)} %get-tuple-element.35, f32[1,32,16,512]{3,2,1,0:T(8,128)S(1)} %get-tuple-element.34), kind=kLoop, calls=%fused_computation | loop fusion | flops 524288 | bytes 4194304 | tf_op jit(solution)/shard_map/stack | solution.py:619
  (15 shorter events, 0.2 us)
Async XLA Ops:
  68.2 2.7 %copy-start = (s32[32]{0:T(128)S(1)}, s32[32]{0:T(128)}, u32[]{:S(2)}) copy-start(s32[32]{0:T(128)} %param.12) | copy-start | bytes 388
where the time goes:
time: 85.7 us; the launch traced here: 85.2 us
  Pallas kernels  65.1 us (76%)
  other arithmetic  10.1 us (12%)
  local copies, waits for them, and re-layouts  9.03 us (11%)
  between operations  0.96 us (1%)
    pallas_call x1, Pallas kernels, slope_pass(): pl.pallas_call(functools.partial(slope_kernel, n_row, n_col, scale), grid...  35.3 us
    pallas_call x1, Pallas kernels, front_pass(): pl.pallas_call(functools.partial(front_kernel, n_row, n_col, own, scale),...  21.7 us
    pallas_call x1, Pallas kernels, back_pass(): pl.pallas_call(back_kernel, grid=(height // (4 * RB),), in_specs=[block,...  8.1 us
    reduce_sum x1, other arithmetic, per_device(): jnp.sum(in_w[0] * all_im[None] - in_w[1] * all_re[None], axis=1)  1.95 us
    reduce_sum x1, other arithmetic, per_device(): jnp.sum(out_w[0] * spec_im[:, None, :] + out_w[1] * spec_re[:, None, :],...  1.95 us

commit v1 on v0

v1 whole, which is shorter than its diff:
```python
import functools
import math

import jax
import jax.numpy as jnp
import ml_dtypes
import numpy as np
from jax import lax
from jax.experimental import pallas as pl
from jax.experimental.pallas import tpu as pltpu
from jax.sharding import PartitionSpec as P

M = 16
A = 2 * M
MODES = A * M
RB = 8
FOLD = 32
F32 = jnp.float32
BF16 = jnp.bfloat16
FULL_TURN = 6.283185307179586
NN = (((1,), (0,)), ((), ()))
NT = (((1,), (1,)), ((), ()))
MIB = 1 << 20
MESH = pl.DeviceIdType.MESH


def trig(frequency, period):
    phases = frequency[:, None] * np.arange(period)[None, :] % period
    angles = phases.astype(np.float32) * np.float32(FULL_TURN / period)
    angles = angles.astype(np.float64)
    return np.cos(angles).astype(np.float32), np.sin(angles).astype(np.float32)


def np_split(x):
    hi = x.astype(ml_dtypes.bfloat16)
    return hi, (x - hi.astype(np.float32)).astype(ml_dtypes.bfloat16)


@functools.lru_cache(maxsize=None)
def tables(n_rows, n_cols):
    frequency = np.arange(A)
    frequency = np.where(frequency < M, frequency, frequency - A)
    rows = np.concatenate(trig(frequency, n_rows), axis=0)
    cos, sin = trig(np.arange(M), n_cols)
    hi, low = np_split(rows)
    rows2 = np.concatenate((hi, low), axis=0)
    rows3 = np.concatenate((hi.T, low.T, hi.T), axis=1)
    hi, low = np_split(np.concatenate((cos, sin), axis=0))
    cols2 = np.concatenate((hi.T, low.T), axis=1)
    hi, low = np_split(np.concatenate((cos, -sin), axis=0))
    wide3 = np.concatenate((hi, hi, low), axis=0)
    return rows2, rows3, cols2, wide3


def split2(x):
    hi = x.astype(BF16)
    return hi, (x - hi.astype(F32)).astype(BF16)


def mm(a, b, dims=NN):
    return lax.dot_general(a, b, dims, preferred_element_type=F32)


def stacked(x, axis):
    hi, low = split2(x)
    return jnp.concatenate((hi.astype(F32), low.astype(F32)), axis=axis).astype(BF16)


def deep_left(x):
    hi = x.astype(BF16).astype(F32)
    return jnp.concatenate((hi, x - hi, hi), axis=1)


def deep_right(x):
    hi = x.astype(BF16).astype(F32)
    return jnp.concatenate((hi, hi, x - hi), axis=0).astype(BF16)


def exact(a, b, dims=NN):
    return lax.dot_general(
        a, b, dims, precision=lax.Precision.HIGHEST, preferred_element_type=F32
    )


def iota(shape, axis):
    return lax.broadcasted_iota(jnp.int32, shape, axis)


def sel(mask):
    return mask.astype(F32)


def pack(dest, vals, out_ref, tiles, cap):
    n = dest.shape[1]
    named = dest == iota((tiles, n), 0)
    before = iota((n, n), 0) < iota((n, n), 1)
    earlier = mm(sel(named).astype(BF16), sel(before).astype(BF16))
    rank = jnp.sum(jnp.where(named, earlier, 0.0), axis=0, keepdims=True)
    position = dest * cap + rank.astype(jnp.int32)
    rows = vals.shape[0]
    hi = vals.astype(BF16)
    left = vals - hi.astype(F32)
    mid = left.astype(BF16)
    low = (left - mid.astype(F32)).astype(BF16)
    parts = jnp.concatenate((hi.astype(F32), mid.astype(F32), low.astype(F32)), axis=0).astype(BF16)
    step = 512
    for first in range(0, tiles * cap, step):
        place = sel(position == iota((step, n), 0) + first).astype(BF16)
        got = mm(parts, place, NT)
        got = got[:rows] + got[rows : 2 * rows] + got[2 * rows : 3 * rows]
        for at in range(0, step, cap):
            out_ref[(first + at) // cap] = got[:, at : at + cap]


def mode_lines(rows2, tall, scale):
    side = tall.shape[1] // 2
    both = mm(rows2, stacked(tall, 1))
    grid = both[: 2 * A, : 2 * side] + both[2 * A :, : 2 * side] + both[: 2 * A, 2 * side :]
    re = (grid[:A, :side] - grid[A:, side:]) * scale
    im = (grid[A:, :side] + grid[:A, side:]) * (-scale)
    return [part[:, at : at + 128] for part in (re, im) for at in range(0, side, 128)]


def as_column(line, first=0, count=None):
    width = line.shape[1]
    shape = (count or width, width)
    picked = jnp.where(iota(shape, 1) == iota(shape, 0) + first, line.astype(F32), 0.0)
    return jnp.sum(picked, axis=1, keepdims=True).astype(jnp.int32)


def same_place():
    return sel(iota((128, 128), 0) % M == iota((128, 128), 1) % M)


def spread8(s8):
    z = jnp.broadcast_to(s8[:, None, :], (8, 8, 128)).reshape(64, 128)
    z = jnp.where(iota((64, 128), 1) // M == iota((64, 128), 0) % 8, z, 0.0)
    z = exact(z, same_place())
    re = jnp.concatenate((z[0:16], z[32:48]), axis=0)
    im = jnp.concatenate((z[16:32], z[48:64]), axis=0)
    return re, im


def compact8(re, im, a):
    y = jnp.concatenate((re, im), axis=0)
    group = iota(y.shape, 1) // M
    y = jnp.where(group == lax.rem(a, 8), y, 0.0)
    y = exact(y, same_place())
    y = jnp.where(group == iota(y.shape, 0) % 8, y, 0.0)
    return jnp.sum(y.reshape(8, 8, 128), axis=1)


def mode_half(re, im, rows3, half_ref):
    grid = jnp.concatenate(
        (jnp.concatenate((re, im), axis=1), jnp.concatenate((-im, re), axis=1)), axis=0
    )
    half = mm(rows3, deep_right(grid))
    side = half.shape[1] // 2
    for o in range(side // M):
        at = o * M
        pair = jnp.concatenate((half[:, at : at + M], half[:, side + at : side + at + M]), axis=1)
        half_ref[o] = deep_left(pair)


def put_tall(tall_ref, first, tall, own):
    for c in range(own):
        for part in range(2):
            at = (part * own + c) * M
            tall_ref[pl.ds(first, RB), at : at + M] = tall[
                c * RB : (c + 1) * RB, part * M : (part + 1) * M
            ]


def col_modes(parts, cols2):
    half = parts.shape[0] // 2
    got = mm(parts, cols2)
    return got[:half, : 2 * M] + got[:half, 2 * M :] + got[half:, : 2 * M]


def main_kernel(
    n_row, n_col, scales,
    dest_ref, cell_ref, res_ref, kept_ref, bias_ref, point_ref, field_ref, w_ref,
    rows2_hbm, rows3_hbm, cols2_hbm, wide3_hbm,
    partial_ref, spec_ref, back_ref, gp_ref,
    rows2_ref, rows3_ref, cols2_ref, wide3_ref, table_sem,
    fbuf, load_sem, wbuf, w_sem, f2_ref, pre_ref, kron2_ref, kronb_ref, tall_ref,
    x1, landed1, send1, gat1, x2, landed2, send2, gat2, rs_send, rs_recv, ag_send, ag_recv,
    grouped, came, trade_send, trade_recv, pts, ids_ref, vm_ref, hot_ref, cot_ref, half_ref,
    sl_ref, other_ref, swap_send, swap_recv, acc_ref, gpx, gpl, gp_send, gp_recv, out_sem,
):
    forward_scale, mix_scale = scales
    n = n_row * n_col
    count = 2 * n
    stride = count // A
    ch = lax.axis_index("ch")
    me = lax.axis_index("row") * n_col + lax.axis_index("col")
    flat = me * 2 + ch
    a = flat // stride
    is_reducer = lax.rem(flat, stride) == 0
    steps, inputs, block, width = fbuf.shape
    own = inputs // 2
    rows = own * RB
    height = steps * block
    subs = block // RB
    points = pts.shape[1]

    def device_of(f):
        p = f // 2
        return (p // n_col, lax.rem(p, n_col), lax.rem(f, 2))

    def remote(src, dst, send, recv, f):
        return pltpu.make_async_remote_copy(
            src_ref=src, dst_ref=dst, send_sem=send, recv_sem=recv,
            device_id=device_of(f), device_id_type=MESH,
        )

    def each(low, high, body):
        def go(k, carry):
            body(k)
            return carry

        lax.fori_loop(low, high, go, 0)

    def on_reducer(body):
        if stride == 1:
            body()
        else:
            pl.when(is_reducer)(body)

    def off_reducer(body):
        if stride > 1:
            pl.when(jnp.logical_not(is_reducer))(body)

    row_at = pl.multiple_of(lax.axis_index("row") * height, 128)
    col_at = pl.multiple_of(lax.axis_index("col") * width, 128)
    table_loads = [
        pltpu.make_async_copy(src, dst, table_sem.at[i])
        for i, (src, dst) in enumerate((
            (rows2_hbm.at[:, pl.ds(row_at, height)], rows2_ref),
            (rows3_hbm.at[pl.ds(row_at, height), :], rows3_ref),
            (cols2_hbm.at[pl.ds(col_at, width), :], cols2_ref),
            (wide3_hbm.at[:, pl.ds(col_at, width)], wide3_ref),
        ))
    ]

    def load(i):
        return pltpu.make_async_copy(
            field_ref.at[:, pl.ds(pl.multiple_of(i * block, block), block), :],
            fbuf.at[i], load_sem.at[i],
        )

    w_load = pltpu.make_async_copy(
        w_ref.at[:, :, :, pl.ds(pl.multiple_of(a // 8 * 128, 128), 128)], wbuf, w_sem
    )
    for one in table_loads:
        one.start()
    each(0, steps, lambda i: load(i).start())
    w_load.start()

    barrier = pltpu.get_barrier_semaphore()
    each(1, count, lambda k: pl.semaphore_signal(
        barrier, inc=1, device_id=device_of(lax.rem(flat + k, count)), device_id_type=MESH
    ))

    shape = (rows, inputs)
    pick = sel(iota(shape, 1) == ch * own + iota(shape, 0) // RB)
    wide_shape = (inputs, inputs * RB)
    spread = sel(iota(wide_shape, 0) == iota(wide_shape, 1) // RB)
    turned = sel(iota(wide_shape, 0) == (iota(wide_shape, 1) // RB + ch * own) % inputs)
    kron_shape = (rows, inputs * RB)
    same = iota(kron_shape, 0) % RB == iota(kron_shape, 1) % RB
    forward_point = exact(exact(pick, point_ref[...], NT), spread)
    kron2_ref[...] = stacked(jnp.where(same, forward_point, 0.0), 0)
    backward_point = exact(exact(pick, point_ref[...]), turned)
    kronb_ref[...] = stacked(jnp.where(same, backward_point, 0.0), 0)
    acc_ref[...] = jnp.zeros_like(acc_ref)
    for one in table_loads:
        one.wait()

    def front(i):
        load(i).wait()
        for u in range(subs):
            b = i * subs + u
            hi, low = split2(fbuf[i, :, u * RB : (u + 1) * RB, :].reshape(inputs * RB, width))
            f2_ref[b, : inputs * RB, :] = hi
            f2_ref[b, inputs * RB :, :] = low
            both = mm(kron2_ref[...], hi)
            pre_ref[b] = both[:rows] + both[rows:] + mm(kron2_ref[:rows, :], low)
            at = pl.multiple_of(ch * rows, rows)
            mine = jnp.concatenate(
                (f2_ref[b, pl.ds(at, rows), :], f2_ref[b, pl.ds(at + inputs * RB, rows), :]), axis=0
            )
            put_tall(tall_ref, pl.multiple_of(b * RB, RB), col_modes(mine, cols2_ref[...]), own)

    each(0, steps, front)

    def scatter(x, landed, stage):
        def copy(k):
            to = lax.rem(a + k, A)
            target = to * stride
            slot = lax.rem(flat - target + count, count)
            return remote(
                x.at[to], landed.at[slot], rs_send.at[stage, k], rs_recv.at[stage], target
            )

        return copy

    def scatter_start(x, landed, stage, scale):
        lines = mode_lines(rows2_ref[...], tall_ref[...], scale)
        for j, line in enumerate(lines):
            x[:, j, :] = line
        copy = scatter(x, landed, stage)
        if stage == 0:
            pl.semaphore_wait(barrier, count - 1)
        each(1, A, lambda k: copy(k).start())
        off_reducer(lambda: copy(0).start())

    def scatter_end(x, landed, stage):
        copy = scatter(x, landed, stage)
        each(1, A, lambda k: copy(k).wait_send())
        off_reducer(lambda: copy(0).wait_send())

    def reduced(x, landed, stage):
        got = landed.at[pl.ds(1, count - 1)]
        remote(got, got, rs_send.at[stage, 0], rs_recv.at[stage], flat).wait_recv()
        pairs = landed[pl.ds(2, count - 2)].reshape(n - 1, 2, 4, 128)
        pairs = jnp.sum(pairs, axis=0)
        mine = x[a] + pairs[0]
        theirs = landed[1] + pairs[1]
        first = jnp.where(ch == 0, mine, theirs)
        second = jnp.where(ch == 0, theirs, mine)
        return jnp.concatenate((first, second), axis=0)

    def gather(source, gat, stage):
        def copy(k):
            f = lax.rem(flat + k, count)
            return remote(
                source.at[lax.rem(ch + k, 2)], gat.at[a], ag_send.at[stage, k],
                ag_recv.at[stage], f,
            )

        return copy

    def gather_wait(gat, stage):
        def take(slots):
            got = gat.at[pl.ds(0, slots)]
            remote(got, got, ag_send.at[stage, 0], ag_recv.at[stage], flat).wait_recv()

        on_reducer(lambda: take(A - 1))
        off_reducer(lambda: take(A))

    def gather_end(source, gat, stage):
        copy = gather(source, gat, stage)
        on_reducer(lambda: each(1, count, lambda k: copy(k).wait_send()))

    rank = jnp.where(a < M, a, A - 1 - a)
    kept = as_column(kept_ref[...])
    allowed = sel((rank < kept) & (iota((inputs, 128), 1) % M < kept))

    scatter_start(x1, landed1, 0, forward_scale)

    cells = (cell_ref[...] + 1).astype(F32)
    vals = jnp.concatenate(
        (res_ref[...], jnp.broadcast_to(cells, (8, cells.shape[1]))), axis=0
    )
    cap = grouped.shape[2]
    pack(dest_ref[...], vals, grouped, n, cap)

    def trade(k):
        p = lax.rem(me + k, n)
        return remote(grouped.at[p], came.at[k], trade_send.at[k], trade_recv, p * 2 + ch)

    each(1, n, lambda k: trade(k).start())
    came[0] = grouped[me]

    def mix():
        s8 = reduced(x1, landed1, 0)
        spec_re, spec_im = spread8(s8)
        w_load.wait()
        re = jnp.zeros((inputs, 128), F32)
        im = jnp.zeros((inputs, 128), F32)
        for c in range(inputs):
            one_re, one_im = spec_re[c : c + 1], spec_im[c : c + 1]
            re = re + (wbuf[0, c] * one_re - wbuf[1, c] * one_im)
            im = im + (wbuf[0, c] * one_im + wbuf[1, c] * one_re)
        keep = allowed * mix_scale
        mixed = compact8(re * keep, im * keep, a)
        for d in range(2):
            send1[d, :8] = s8
            send1[d, 8:10] = mixed[2 * d : 2 * d + 2]
            send1[d, 10:12] = mixed[4 + 2 * d : 6 + 2 * d]
        copy = gather(send1, gat1, 0)
        each(1, count, lambda k: copy(k).start())
        gat1[a] = send1[ch]

    on_reducer(mix)
    if stride > 1:
        off_reducer(lambda: w_load.wait())

    came_all = came.at[pl.ds(1, n - 1)]
    remote(came_all, came_all, trade_send.at[0], trade_recv, flat).wait_recv()
    for p in range(n):
        pts[:, p * cap : (p + 1) * cap] = came[p]
    cell = pts[own : own + 1, :].astype(jnp.int32) - 1
    row = cell // width
    fold = jnp.where(cell < 0, -1, row % FOLD)
    code = jnp.where(cell < 0, -1, row // FOLD * width + cell % width).astype(F32)
    for first in range(0, points, 128):
        ids_ref[first : first + 128, :] = jnp.broadcast_to(
            code[:, first : first + 128], (128, 128)
        ).T
    here = fold == iota((FOLD, points), 0)
    half_own = own // 2

    def fill(o):
        value = pts[pl.ds(o, 1), :]
        hi = value.astype(BF16).astype(F32)
        group = o // half_own
        at = pl.multiple_of(lax.rem(o, half_own) * FOLD, FOLD)
        vm_ref[group, pl.ds(at, FOLD), :] = jnp.where(here, hi, 0.0).astype(BF16)
        vm_ref[group, pl.ds(at + half_own * FOLD, FOLD), :] = jnp.where(
            here, value - hi, 0.0
        ).astype(BF16)

    each(0, own, fill)
    span = half_own * FOLD

    def place(q):
        for at in range(0, width, 128):
            names = (iota((points, 128), 1) + (q * width + at)).astype(F32)
            hot_ref[:, at : at + 128] = sel(ids_ref[...] == names).astype(BF16)
        for group in range(2):
            got = mm(vm_ref[group], hot_ref[...])
            got = (got[:span] + got[span:]).reshape(half_own, FOLD, width)
            cot_ref[
                group * half_own : (group + 1) * half_own,
                pl.ds(pl.multiple_of(q * FOLD, FOLD), FOLD), :,
            ] = got

    each(0, height // FOLD, place)

    gather_wait(gat1, 0)
    re = jnp.concatenate((gat1[:, 8, :], gat1[:, 9, :]), axis=1)
    im = jnp.concatenate((gat1[:, 10, :], gat1[:, 11, :]), axis=1)
    bias_shape = (own, own * M)
    bias_at = sel(iota(bias_shape, 1) == iota(bias_shape, 0) * M)
    bias_line = exact(jnp.broadcast_to(bias_ref[...], (8, own)), bias_at)[:1]
    re = re + jnp.where(iota(re.shape, 0) == 0, bias_line, 0.0)
    mode_half(re, im, rows3_ref[...], half_ref)

    def swap(i):
        at = pl.ds(i * subs, subs)
        return remote(
            pre_ref.at[at], other_ref.at[at], swap_send.at[i], swap_recv.at[i], me * 2 + 1 - ch
        )

    k0 = math.sqrt(2.0 / math.pi)

    def slopes(i):
        for u in range(subs):
            b = i * subs + u
            first = pl.multiple_of(b * RB, RB)
            half = half_ref[:, pl.ds(first, RB), :].reshape(rows, 6 * M).astype(BF16)
            pre = pre_ref[b] + mm(half, wide3_ref[...])
            cot = cot_ref[:, pl.ds(first, RB), :].reshape(rows, width)
            square = pre * pre
            t = jnp.tanh(k0 * pre * (1.0 + 0.044715 * square))
            rate = 0.5 * (1.0 + t) + 0.5 * k0 * pre * (1.0 - t * t) * (1.0 + 3 * 0.044715 * square)
            slope = cot * rate
            pre_ref[b] = slope
            hi, low = split2(slope)
            sl_ref[b, :rows, :] = hi
            sl_ref[b, rows:, :] = low
            put_tall(tall_ref, first, col_modes(sl_ref[b], cols2_ref[...]), own)
        swap(i).start()

    each(0, steps, slopes)
    scatter_start(x2, landed2, 1, mix_scale)

    def point_sums(i):
        fields = jnp.concatenate([f2_ref[i * 2 + u] for u in range(2)], axis=1)
        found = jnp.concatenate([sl_ref[i * 2 + u] for u in range(2)], axis=1)
        acc_ref[...] += mm(fields, found, NT)

    each(0, steps * subs // 2, point_sums)
    total = acc_ref[: inputs * RB, :] + acc_ref[inputs * RB :, :]
    total = total[:, :rows] + total[:, rows:]
    matched = iota(total.shape, 0) % RB == iota(total.shape, 1) % RB
    total = jnp.sum(jnp.where(matched, total, 0.0).reshape(inputs, RB, rows), axis=1)
    into = 128 // own
    group = sel(iota((rows, 128), 0) // RB == iota((rows, 128), 1) % own)
    total = exact(total, group)
    mine = iota(total.shape, 1) // own == iota(total.shape, 0) % into
    gpx[...] = jnp.sum(jnp.where(mine, total, 0.0).reshape(inputs // into, into, 128), axis=1)

    def point_send(k):
        p = lax.rem(me + k, n)
        return remote(gpx, gpl.at[k], gp_send.at[k], gp_recv, p * 2 + ch)

    each(1, n, lambda k: point_send(k).start())

    def adjoint():
        s8 = reduced(x2, landed2, 1)
        grad_re, grad_im = spread8(s8)
        grad_re = grad_re * allowed
        grad_im = grad_im * allowed
        lines_re, lines_im = [], []
        for c in range(inputs):
            w_re, w_im = wbuf[0, c], wbuf[1, c]
            lines_re.append(jnp.sum(w_re * grad_re + w_im * grad_im, axis=0, keepdims=True))
            lines_im.append(jnp.sum(w_re * grad_im - w_im * grad_re, axis=0, keepdims=True))
        re = jnp.concatenate(lines_re, axis=0) * forward_scale
        im = jnp.concatenate(lines_im, axis=0) * forward_scale
        turned_modes = compact8(re, im, a)
        for d in range(2):
            send2[d, :2] = turned_modes[2 * d : 2 * d + 2]
            send2[d, 2:4] = turned_modes[4 + 2 * d : 6 + 2 * d]
            send2[d, 4:8] = s8[4 * d : 4 * d + 4]
        copy = gather(send2, gat2, 1)
        each(1, count, lambda k: copy(k).start())
        gat2[a] = send2[ch]

    on_reducer(adjoint)

    def store(i):
        at = pl.ds(pl.multiple_of(i * block, block), block)
        return pltpu.make_async_copy(cot_ref.at[:, at, :], partial_ref.at[:, at, :], out_sem.at[i])

    def backs(i):
        swap(i).wait_recv()
        for u in range(subs):
            b = i * subs + u
            first = pl.multiple_of(b * RB, RB)
            other_hi, other_low = split2(other_ref[b])
            hi = jnp.concatenate((sl_ref[b, :rows, :], other_hi), axis=0)
            low = jnp.concatenate((sl_ref[b, rows:, :], other_low), axis=0)
            both = mm(kronb_ref[...], hi)
            result = both[:rows] + both[rows:] + mm(kronb_ref[:rows, :], low)
            cot_ref[:, pl.ds(first, RB), :] = result.reshape(own, RB, width)
        store(i).start()

    each(0, steps, backs)

    gp_all = gpl.at[pl.ds(1, n - 1)]
    remote(gp_all, gp_all, gp_send.at[0], gp_recv, flat).wait_recv()
    gp_ref[...] = gpx[...] + jnp.sum(gpl[pl.ds(1, n - 1)], axis=0)
    gather_wait(gat2, 1)
    spec_ref[...] = gat1[...]
    back_ref[...] = gat2[...]

    scatter_end(x1, landed1, 0)
    scatter_end(x2, landed2, 1)
    gather_end(send1, gat1, 0)
    gather_end(send2, gat2, 1)
    each(1, n, lambda k: trade(k).wait_send())
    each(1, n, lambda k: point_send(k).wait_send())
    each(0, steps, lambda i: swap(i).wait_send())
    each(0, steps, lambda i: store(i).wait())


def main_pass(args, constants, scales, cap, n_row, n_col):
    field = args[6]
    n = n_row * n_col
    count = 2 * n
    inputs, height, width = field.shape
    own = inputs // 2
    block = 2 * RB
    steps = height // block
    blocks = height // RB
    rows = own * RB
    kept = own + 8
    points = n * cap
    vmem = pl.BlockSpec(memory_space=pltpu.VMEM)
    hbm = pl.BlockSpec(memory_space=pl.ANY)
    dma = pltpu.SemaphoreType.DMA
    rows2, rows3, cols2, wide3 = constants
    return pl.pallas_call(
        functools.partial(main_kernel, n_row, n_col, scales),
        out_shape=[
            jax.ShapeDtypeStruct((own, height, width), F32),
            jax.ShapeDtypeStruct((A, 12, 128), F32),
            jax.ShapeDtypeStruct((A, 8, 128), F32),
            jax.ShapeDtypeStruct((4, 128), F32),
        ],
        in_specs=[vmem] * 6 + [hbm] * 6,
        out_specs=[hbm, vmem, vmem, vmem],
        scratch_shapes=[
            pltpu.VMEM((rows2.shape[0], height), BF16),
            pltpu.VMEM((height, rows3.shape[1]), BF16),
            pltpu.VMEM((width, cols2.shape[1]), BF16),
            pltpu.VMEM((wide3.shape[0], width), BF16),
            dma((4,)),
            pltpu.VMEM((steps, inputs, block, width), F32),
            dma((steps,)),
            pltpu.VMEM((2, inputs, inputs, 128), F32),
            dma,
            pltpu.VMEM((blocks, 2 * inputs * RB, width), BF16),
            pltpu.VMEM((blocks, rows, width), F32),
            pltpu.VMEM((2 * rows, inputs * RB), BF16),
            pltpu.VMEM((2 * rows, inputs * RB), BF16),
            pltpu.VMEM((height, 2 * own * M), F32),
            pltpu.VMEM((A, 4, 128), F32),
            pltpu.VMEM((count, 4, 128), F32),
            pltpu.VMEM((2, 12, 128), F32),
            pltpu.VMEM((A, 12, 128), F32),
            pltpu.VMEM((A, 4, 128), F32),
            pltpu.VMEM((count, 4, 128), F32),
            pltpu.VMEM((2, 8, 128), F32),
            pltpu.VMEM((A, 8, 128), F32),
            dma((2, A)),
            dma((2,)),
            dma((2, count)),
            dma((2,)),
            pltpu.VMEM((n, kept, cap), F32),
            pltpu.VMEM((n, kept, cap), F32),
            dma((n,)),
            dma,
            pltpu.VMEM((kept, points), F32),
            pltpu.VMEM((points, 128), F32),
            pltpu.VMEM((2, own * FOLD, points), BF16),
            pltpu.VMEM((points, width), BF16),
            pltpu.VMEM((own, height, width), F32),
            pltpu.VMEM((own, height, 6 * M), F32),
            pltpu.VMEM((blocks, 2 * rows, width), BF16),
            pltpu.VMEM((blocks, rows, width), F32),
            dma((steps,)),
            dma((steps,)),
            pltpu.VMEM((2 * inputs * RB, 2 * rows), F32),
            pltpu.VMEM((4, 128), F32),
            pltpu.VMEM((n, 4, 128), F32),
            dma((n,)),
            dma,
            dma((steps,)),
        ],
        compiler_params=pltpu.CompilerParams(
            collective_id=0, has_side_effects=True, vmem_limit_bytes=58 * MIB
        ),
    )(*args, *constants)


def turn_blocks(x):
    group = iota((8, 128), 1) // M
    line = iota((8, 128), 0)
    out = jnp.where(group == line, x, 0.0)
    for d in range(1, 8):
        y = pltpu.roll(pltpu.roll(x, d * M, 1), 8 - d, 0)
        out = jnp.where((group - line + 8) % 8 == d, y, out)
    return out


def back_kernel(
    scales, partial_ref, spec_ref, back_ref, gp_ref, kept_ref, rows3_hbm, wide3_hbm,
    out_ref, gs_ref, point_ref, bias_ref,
    half_ref, spec_t, grad_t, point_t, rows3_ref, wide3_ref, table_sem,
):
    grad_scale, norm_points, bias_scale = scales
    step = pl.program_id(0)
    own, block, width = out_ref.shape
    rows = own * RB
    height = half_ref.shape[1]
    each = gs_ref.shape[1]
    inputs = 2 * own

    @pl.when(step == 0)
    def _():
        row_at = pl.multiple_of(lax.axis_index("row") * height, 128)
        col_at = pl.multiple_of(lax.axis_index("col") * width, 128)
        loads = [
            pltpu.make_async_copy(
                rows3_hbm.at[pl.ds(row_at, height), :], rows3_ref, table_sem.at[0]
            ),
            pltpu.make_async_copy(
                wide3_hbm.at[:, pl.ds(col_at, width)], wide3_ref, table_sem.at[1]
            ),
        ]
        for one in loads:
            one.start()
        kept = as_column(kept_ref[...], lax.axis_index("ch") * own, own)
        mode = iota((own, MODES), 1)
        row_mode = mode // M
        rank = jnp.where(row_mode < M, row_mode, A - 1 - row_mode)
        keep = jnp.where((rank < kept) & (mode % M < kept), grad_scale, 0.0)
        biases = jnp.zeros((1, own), F32)
        for part in range(2):
            for octet in range(own // 8):
                j = part * (own // 8) + octet
                for t in range(A // 8):
                    lanes = slice(t * 128, (t + 1) * 128)
                    lines = slice(octet * 8, octet * 8 + 8)
                    got = turn_blocks(back_ref[t * 8 : t * 8 + 8, 4 + j, :])
                    if part == 0 and t == 0:
                        shape = (8, own)
                        named = iota(shape, 1) == iota(shape, 0) + octet * 8
                        named = jnp.where(named, got[:, :1] * bias_scale, 0.0)
                        biases = biases + jnp.sum(named, axis=0, keepdims=True)
                    grad_t[part, lines, lanes] = got * keep[lines, lanes]
                    for side in range(2):
                        at = side * own + octet * 8
                        spec_t[part, at : at + 8, lanes] = turn_blocks(
                            spec_ref[t * 8 : t * 8 + 8, side * 4 + j, :]
                        )
        bias_ref[...] = biases
        gp = gp_ref[...] * norm_points
        into = 128 // own
        for k in range(into):
            for i in range(inputs // into):
                at = i * into + k
                point_t[at : at + 1, :] = gp[i : i + 1, k * own : (k + 1) * own]
        eye = sel(iota((own, own), 0) == iota((own, own), 1))
        point_ref[...] = exact(eye, point_t[...], NT)
        for one in loads:
            one.wait()
        re = jnp.concatenate((back_ref[:, 0, :], back_ref[:, 1, :]), axis=1)
        im = jnp.concatenate((back_ref[:, 2, :], back_ref[:, 3, :]), axis=1)
        mode_half(re, im, rows3_ref[...], half_ref)

    for u in range(block // RB):
        at = slice(u * RB, (u + 1) * RB)
        first = pl.multiple_of(step * block + u * RB, RB)
        half = half_ref[:, pl.ds(first, RB), :].reshape(rows, 6 * M).astype(BF16)
        result = mm(half, wide3_ref[...]).reshape(own, RB, width)
        out_ref[:, at, :] = partial_ref[:, at, :] + result
    for i in range(each):
        c = step * each + i
        spec_re = spec_t[0, pl.ds(c, 1), :]
        spec_im = spec_t[1, pl.ds(c, 1), :]
        gs_ref[0, i] = grad_t[0] * spec_re + grad_t[1] * spec_im
        gs_ref[1, i] = grad_t[1] * spec_re - grad_t[0] * spec_im


def whole(shape):
    return pl.BlockSpec(shape, lambda i: (0,) * len(shape))


def back_pass(partial, spec, back, gp, kept, rows3, wide3, scales):
    own, height, width = partial.shape
    block = 4 * RB
    steps = height // block
    each = 2 * own // steps
    hbm = pl.BlockSpec(memory_space=pl.ANY)
    tile = pl.BlockSpec((own, block, width), lambda i: (0, i, 0))
    return pl.pallas_call(
        functools.partial(back_kernel, scales),
        grid=(steps,),
        in_specs=[tile, whole(spec.shape), whole(back.shape), whole(gp.shape), whole(kept.shape)]
        + [hbm, hbm],
        out_specs=[
            tile,
            pl.BlockSpec((2, each, own, MODES), lambda i: (0, i, 0, 0)),
            whole((own, 2 * own)),
            whole((1, own)),
        ],
        out_shape=[
            jax.ShapeDtypeStruct((own, height, width), F32),
            jax.ShapeDtypeStruct((2, 2 * own, own, MODES), F32),
            jax.ShapeDtypeStruct((own, 2 * own), F32),
            jax.ShapeDtypeStruct((1, own), F32),
        ],
        scratch_shapes=[
            pltpu.VMEM((own, height, 6 * M), F32),
            pltpu.VMEM((2, 2 * own, MODES), F32),
            pltpu.VMEM((2, own, MODES), F32),
            pltpu.VMEM((2 * own, own), F32),
            pltpu.VMEM((height, rows3.shape[1]), BF16),
            pltpu.VMEM((wide3.shape[0], width), BF16),
            pltpu.SemaphoreType.DMA((2,)),
        ],
        compiler_params=pltpu.CompilerParams(vmem_limit_bytes=58 * MIB),
    )(partial, spec, back, gp, kept, rows3, wide3)


def per_device(
    field, spec_weight, point_weight, bias, kept_modes, residual, trace_dest, trace_cell
):
    n_row = lax.axis_size("row")
    n_col = lax.axis_size("col")
    inputs, height, width = field.shape
    own = inputs // lax.axis_size("ch")
    points = trace_dest.shape[0]
    tiles = n_row * n_col
    points_all = points * tiles
    cap = max(2, 2 * points // tiles)
    forward_scale = 1.0 / math.sqrt(height * n_row * width * n_col)
    mix_scale = 1.0 / math.sqrt(MODES)
    norm_points = 1.0 / math.sqrt(points_all)
    constants = [jnp.asarray(t) for t in tables(height * n_row, width * n_col)]
    kept = kept_modes.reshape(1, inputs)
    args = (
        trace_dest.reshape(1, points), trace_cell.reshape(1, points), residual, kept,
        bias.reshape(1, own), point_weight, field, spec_weight,
    )
    partial, spec, back, gp = main_pass(
        args, constants, (forward_scale, mix_scale), cap, n_row, n_col
    )
    grad_field, grad_spec, grad_point, grad_bias = back_pass(
        partial, spec, back, gp, kept, constants[1], constants[3],
        (math.sqrt(MODES / points_all), norm_points, norm_points / mix_scale),
    )
    return (grad_field, grad_spec, grad_point.T, grad_bias.reshape(own))


def solution(mesh):
    return jax.shard_map(
        per_device,
        mesh=mesh,
        in_specs=(
            P(None, "row", "col"),
            P(),
            P(),
            P("ch"),
            P(),
            P("ch", ("row", "col")),
            P(("row", "col"), None),
            P(("row", "col")),
        ),
        out_specs=(P("ch", "row", "col"), P(None, None, "ch", None), P(None, "ch"), P("ch")),
        check_vma=False,
    )
```

time: 85.7 us -> 68.1 us (0.79)
  other arithmetic: 10.1 us -> 0 us
  local copies, waits for them, and re-layouts: 9.03 us -> 0 us
  Pallas kernels: 65.1 us -> 67.1 us
    reduce_sum x2 -> x0, other arithmetic: 3.9 us -> none  [the longest x1 1.95 us: per_device(): jnp.sum(in_w[0] * all_im[None] - in_w[1] * all_re[None], axis=1)]
    pallas_call x3 -> x2, Pallas kernels: 65.1 us -> 67.1 us  [the longest x1 58.1 us: main_pass(): pl.pallas_call(functools.partial(main_kernel, n_row, n_col, scales), out_...]
    dynamic_slice x2 -> x0, local copies, waits for them, and re-layouts: 1.66 us -> none  [the longest x1 0.87 us: per_device(): lax.dynamic_slice_in_dim(own_point, first, own, 1)]
    unnamed x5 -> x0, local copies, waits for them, and re-layouts: 1.66 us -> none
    another operation x1 -> x0, other arithmetic: 1.58 us -> none  [per_device(): jnp.stack((keep_re[None] * spec_re[:, None] + keep_im[None] * spec_im[:,...]
    reshape x7 -> x0, local copies, waits for them, and re-layouts: 1.56 us -> none  [the longest x1 0.63 us: unfold(): return lines.reshape(2, 2 * own, MODES)]
    concatenate x6 -> x0, other arithmetic: 1.52 us -> none  [the longest x1 0.94 us: per_device(): jnp.concatenate((residual, (trace_cell + 1).astype(F32)[None, :], jnp.zer...]
    slice x9 -> x0, local copies, waits for them, and re-layouts: 1.11 us -> none  [the longest x3 0.75 us: per_device(): modes_re, modes_im = (modes[0], modes[1])]
where the time goes in v1:
time: 68.1 us; the launch traced here: 67.8 us
  Pallas kernels  67.1 us (99%)
    pallas_call x1, Pallas kernels, main_pass(): pl.pallas_call(functools.partial(main_kernel, n_row, n_col, scales), out_...  58.1 us
    pallas_call x1, Pallas kernels, back_pass(): pl.pallas_call(functools.partial(back_kernel, scales), grid=(steps,), in_...  9.01 us

profile of v1, /device:TPU:0, one launch (start us, length us, event | category | flops | bytes accessed | tf_op | source)
XLA Modules:
  0.0 67.8 jit_solution(13108998880911046266)
XLA Ops:
  0.6 58.1 %shard_map.147 = (f32[16,128,512]{2,1,0:T(8,128)}, f32[32,12,128]{2,1,0:T(8,128)}, f32[32,8,128]{2,1,0:T(8,128)}, f32[4,128]{1,0:T(4,128)}) custom-call(s32[1,1024]{1,0:T(1,128)} %bitcast.6, s32[1,1024]{1,0:T(1,128)} %bitcast.7, f32[16,1024]{1,0:T(8,128)} %res_ref.1, s32[1,32]{1,0:T(1,128)} %bitcast.8, f32[1,16]{1,0:T(1,128)} %bitcast.10, ...), custom_call_target="tpu_custom_call" | custom-call | tf_op jit(solution)/shard_map/pallas_call | solution.py:577
  58.8 9.0 %shard_map.148 = (f32[16,128,512]{2,1,0:T(8,128)}, f32[2,32,16,512]{3,2,1,0:T(8,128)}, f32[16,32]{1,0:T(8,128)}, f32[1,16]{1,0:T(1,128)}) custom-call(f32[16,128,512]{2,1,0:T(8,128)} %get-tuple-element.12.partial_ref, f32[32,12,128]{2,1,0:T(8,128)} %get-tuple-element.13.spec_ref, f32[32,8,128]{2,1,0:T(8,128)} %get-tuple-element.14.back_ref, ...), custom_call_target="tpu_custom_call" | custom-call | tf_op jit(solution)/shard_map/pallas_call | solution.py:742

commit v2 on v1

--- a/solution.py
+++ b/solution.py
@@ -121,6 +121,18 @@
     return [part[:, at : at + 128] for part in (re, im) for at in range(0, side, 128)]
 
 
+def part_of(x, size):
+    if size & (size - 1) == 0:
+        return lax.shift_right_logical(x, size.bit_length() - 1)
+    return lax.div(x, size)
+
+
+def rest_of(x, size):
+    if size & (size - 1) == 0:
+        return x & (size - 1)
+    return lax.rem(x, size)
+
+
 def as_column(line, first=0, count=None):
     width = line.shape[1]
     shape = (count or width, width)
@@ -195,8 +207,9 @@
     ch = lax.axis_index("ch")
     me = lax.axis_index("row") * n_col + lax.axis_index("col")
     flat = me * 2 + ch
-    a = flat // stride
-    is_reducer = lax.rem(flat, stride) == 0
+    a = part_of(flat, stride)
+    is_reducer = rest_of(flat, stride) == 0
+    small = stride == 1
     steps, inputs, block, width = fbuf.shape
     own = inputs // 2
     rows = own * RB
@@ -205,14 +218,22 @@
     points = pts.shape[1]
 
     def device_of(f):
-        p = f // 2
-        return (p // n_col, lax.rem(p, n_col), lax.rem(f, 2))
+        f = jnp.int32(f)
+        p = part_of(f, 2)
+        return (part_of(p, n_col), rest_of(p, n_col), rest_of(f, 2))
 
     def remote(src, dst, send, recv, f):
         return pltpu.make_async_remote_copy(
             src_ref=src, dst_ref=dst, send_sem=send, recv_sem=recv,
             device_id=device_of(f), device_id_type=MESH,
         )
+
+    def some(low, high, body):
+        if small:
+            for k in range(low, high):
+                body(k)
+        else:
+            each(low, high, body)
 
     def each(low, high, body):
         def go(k, carry):
@@ -250,7 +271,7 @@
         )
 
     w_load = pltpu.make_async_copy(
-        w_ref.at[:, :, :, pl.ds(pl.multiple_of(a // 8 * 128, 128), 128)], wbuf, w_sem
+        w_ref.at[:, :, :, pl.ds(pl.multiple_of(part_of(a, 8) * 128, 128), 128)], wbuf, w_sem
     )
     for one in table_loads:
         one.start()
@@ -258,8 +279,8 @@
     w_load.start()
 
     barrier = pltpu.get_barrier_semaphore()
-    each(1, count, lambda k: pl.semaphore_signal(
-        barrier, inc=1, device_id=device_of(lax.rem(flat + k, count)), device_id_type=MESH
+    some(1, count, lambda k: pl.semaphore_signal(
+        barrier, inc=1, device_id=device_of(rest_of(flat + k, count)), device_id_type=MESH
     ))
 
     shape = (rows, inputs)
@@ -296,11 +317,11 @@
 
     def scatter(x, landed, stage):
         def copy(k):
-            to = lax.rem(a + k, A)
+            to = rest_of(a + k, A)
             target = to * stride
-            slot = lax.rem(flat - target + count, count)
+            slot = count - k if small else rest_of(flat - target + count, count)
             return remote(
-                x.at[to], landed.at[slot], rs_send.at[stage, k], rs_recv.at[stage], target
+                x.at[to], landed.at[slot], rs_send.at[stage], rs_recv.at[stage], target
             )
 
         return copy
@@ -312,17 +333,20 @@
         copy = scatter(x, landed, stage)
         if stage == 0:
             pl.semaphore_wait(barrier, count - 1)
-        each(1, A, lambda k: copy(k).start())
+        some(1, A, lambda k: copy(k).start())
         off_reducer(lambda: copy(0).start())
 
     def scatter_end(x, landed, stage):
-        copy = scatter(x, landed, stage)
-        each(1, A, lambda k: copy(k).wait_send())
-        off_reducer(lambda: copy(0).wait_send())
+        def take(slots):
+            sent = x.at[pl.ds(0, slots)]
+            remote(sent, sent, rs_send.at[stage], rs_recv.at[stage], flat).wait_send()
+
+        on_reducer(lambda: take(A - 1))
+        off_reducer(lambda: take(A))
 
     def reduced(x, landed, stage):
         got = landed.at[pl.ds(1, count - 1)]
-        remote(got, got, rs_send.at[stage, 0], rs_recv.at[stage], flat).wait_recv()
+        remote(got, got, rs_send.at[stage], rs_recv.at[stage], flat).wait_recv()
         pairs = landed[pl.ds(2, count - 2)].reshape(n - 1, 2, 4, 128)
         pairs = jnp.sum(pairs, axis=0)
         mine = x[a] + pairs[0]
@@ -333,10 +357,10 @@
 
     def gather(source, gat, stage):
         def copy(k):
-            f = lax.rem(flat + k, count)
+            f = rest_of(flat + k, count)
+            send = ag_send.at[stage, 0 if small else k]
             return remote(
-                source.at[lax.rem(ch + k, 2)], gat.at[a], ag_send.at[stage, k],
-                ag_recv.at[stage], f,
+                source.at[rest_of(ch + k, 2)], gat.at[a], send, ag_recv.at[stage], f
             )
 
         return copy
@@ -350,8 +374,12 @@
         off_reducer(lambda: take(A))
 
     def gather_end(source, gat, stage):
-        copy = gather(source, gat, stage)
-        on_reducer(lambda: each(1, count, lambda k: copy(k).wait_send()))
+        if small:
+            sent = gat.at[pl.ds(0, A - 1)]
+            remote(sent, sent, ag_send.at[stage, 0], ag_recv.at[stage], flat).wait_send()
+        else:
+            copy = gather(source, gat, stage)
+            on_reducer(lambda: each(1, count, lambda k: copy(k).wait_send()))
 
     rank = jnp.where(a < M, a, A - 1 - a)
     kept = as_column(kept_ref[...])
@@ -367,10 +395,10 @@
     pack(dest_ref[...], vals, grouped, n, cap)
 
     def trade(k):
-        p = lax.rem(me + k, n)
-        return remote(grouped.at[p], came.at[k], trade_send.at[k], trade_recv, p * 2 + ch)
-
-    each(1, n, lambda k: trade(k).start())
+        p = rest_of(me + k, n)
+        return remote(grouped.at[p], came.at[k], trade_send, trade_recv, p * 2 + ch)
+
+    some(1, n, lambda k: trade(k).start())
     came[0] = grouped[me]
 
     def mix():
@@ -390,7 +418,7 @@
             send1[d, 8:10] = mixed[2 * d : 2 * d + 2]
             send1[d, 10:12] = mixed[4 + 2 * d : 6 + 2 * d]
         copy = gather(send1, gat1, 0)
-        each(1, count, lambda k: copy(k).start())
+        some(1, count, lambda k: copy(k).start())
         gat1[a] = send1[ch]
 
     on_reducer(mix)
@@ -398,7 +426,7 @@
         off_reducer(lambda: w_load.wait())
 
     came_all = came.at[pl.ds(1, n - 1)]
-    remote(came_all, came_all, trade_send.at[0], trade_recv, flat).wait_recv()
+    remote(came_all, came_all, trade_send, trade_recv, flat).wait_recv()
     for p in range(n):
         pts[:, p * cap : (p + 1) * cap] = came[p]
     cell = pts[own : own + 1, :].astype(jnp.int32) - 1
@@ -451,7 +479,7 @@
     def swap(i):
         at = pl.ds(i * subs, subs)
         return remote(
-            pre_ref.at[at], other_ref.at[at], swap_send.at[i], swap_recv.at[i], me * 2 + 1 - ch
+            pre_ref.at[at], other_ref.at[at], swap_send, swap_recv.at[i], me * 2 + 1 - ch
         )
 
     k0 = math.sqrt(2.0 / math.pi)
@@ -494,10 +522,10 @@
     gpx[...] = jnp.sum(jnp.where(mine, total, 0.0).reshape(inputs // into, into, 128), axis=1)
 
     def point_send(k):
-        p = lax.rem(me + k, n)
-        return remote(gpx, gpl.at[k], gp_send.at[k], gp_recv, p * 2 + ch)
-
-    each(1, n, lambda k: point_send(k).start())
+        p = rest_of(me + k, n)
+        return remote(gpx, gpl.at[k], gp_send, gp_recv, p * 2 + ch)
+
+    some(1, n, lambda k: point_send(k).start())
 
     def adjoint():
         s8 = reduced(x2, landed2, 1)
@@ -517,14 +545,14 @@
             send2[d, 2:4] = turned_modes[4 + 2 * d : 6 + 2 * d]
             send2[d, 4:8] = s8[4 * d : 4 * d + 4]
         copy = gather(send2, gat2, 1)
-        each(1, count, lambda k: copy(k).start())
+        some(1, count, lambda k: copy(k).start())
         gat2[a] = send2[ch]
 
     on_reducer(adjoint)
 
     def store(i):
         at = pl.ds(pl.multiple_of(i * block, block), block)
-        return pltpu.make_async_copy(cot_ref.at[:, at, :], partial_ref.at[:, at, :], out_sem.at[i])
+        return pltpu.make_async_copy(cot_ref.at[:, at, :], partial_ref.at[:, at, :], out_sem)
 
     def backs(i):
         swap(i).wait_recv()
@@ -542,7 +570,7 @@
     each(0, steps, backs)
 
     gp_all = gpl.at[pl.ds(1, n - 1)]
-    remote(gp_all, gp_all, gp_send.at[0], gp_recv, flat).wait_recv()
+    remote(gp_all, gp_all, gp_send, gp_recv, flat).wait_recv()
     gp_ref[...] = gpx[...] + jnp.sum(gpl[pl.ds(1, n - 1)], axis=0)
     gather_wait(gat2, 1)
     spec_ref[...] = gat1[...]
@@ -552,10 +580,11 @@
     scatter_end(x2, landed2, 1)
     gather_end(send1, gat1, 0)
     gather_end(send2, gat2, 1)
-    each(1, n, lambda k: trade(k).wait_send())
-    each(1, n, lambda k: point_send(k).wait_send())
-    each(0, steps, lambda i: swap(i).wait_send())
-    each(0, steps, lambda i: store(i).wait())
+    remote(came_all, came_all, trade_send, trade_recv, flat).wait_send()
+    remote(gp_all, gp_all, gp_send, gp_recv, flat).wait_send()
+    sent = pre_ref.at[pl.ds(0, steps * subs)]
+    remote(sent, sent, swap_send, swap_recv.at[0], flat).wait_send()
+    pltpu.make_async_copy(cot_ref, partial_ref, out_sem).wait()
 
 
 def main_pass(args, constants, scales, cap, n_row, n_col):
@@ -607,13 +636,13 @@
             pltpu.VMEM((count, 4, 128), F32),
             pltpu.VMEM((2, 8, 128), F32),
             pltpu.VMEM((A, 8, 128), F32),
-            dma((2, A)),
+            dma((2,)),
             dma((2,)),
             dma((2, count)),
             dma((2,)),
             pltpu.VMEM((n, kept, cap), F32),
             pltpu.VMEM((n, kept, cap), F32),
-            dma((n,)),
+            dma,
             dma,
             pltpu.VMEM((kept, points), F32),
             pltpu.VMEM((points, 128), F32),
@@ -623,14 +652,14 @@
             pltpu.VMEM((own, height, 6 * M), F32),
             pltpu.VMEM((blocks, 2 * rows, width), BF16),
             pltpu.VMEM((blocks, rows, width), F32),
-            dma((steps,)),
+            dma,
             dma((steps,)),
             pltpu.VMEM((2 * inputs * RB, 2 * rows), F32),
             pltpu.VMEM((4, 128), F32),
             pltpu.VMEM((n, 4, 128), F32),
-            dma((n,)),
             dma,
-            dma((steps,)),
+            dma,
+            dma,
         ],
         compiler_params=pltpu.CompilerParams(
             collective_id=0, has_side_effects=True, vmem_limit_bytes=58 * MIB

time: 68.1 us -> 64.3 us (0.944)
  Pallas kernels: 67.1 us -> 63.4 us
    pallas_call x1, Pallas kernels: 58.1 us -> 54.4 us  [main_pass(): pl.pallas_call(functools.partial(main_kernel, n_row, n_col, scales), out_...]
where the time goes in v2:
time: 64.3 us; the launch traced here: 64.1 us
  Pallas kernels  63.4 us (99%)
    pallas_call x1, Pallas kernels, main_pass(): pl.pallas_call(functools.partial(main_kernel, n_row, n_col, scales), out_...  54.4 us
    pallas_call x1, Pallas kernels, back_pass(): pl.pallas_call(functools.partial(back_kernel, scales), grid=(steps,), in_...  9.01 us

profile of v2, /device:TPU:0, one launch (start us, length us, event | category | flops | bytes accessed | tf_op | source)
XLA Modules:
  0.0 64.1 jit_solution(1142895522019429885)
XLA Ops:
  0.6 54.4 %shard_map.147 = (f32[16,128,512]{2,1,0:T(8,128)}, f32[32,12,128]{2,1,0:T(8,128)}, f32[32,8,128]{2,1,0:T(8,128)}, f32[4,128]{1,0:T(4,128)}) custom-call(s32[1,1024]{1,0:T(1,128)} %bitcast.6, s32[1,1024]{1,0:T(1,128)} %bitcast.7, f32[16,1024]{1,0:T(8,128)} %res_ref.1, s32[1,32]{1,0:T(1,128)} %bitcast.8, f32[1,16]{1,0:T(1,128)} %bitcast.10, ...), custom_call_target="tpu_custom_call" | custom-call | tf_op jit(solution)/shard_map/pallas_call | solution.py:606
  55.0 9.0 %shard_map.148 = (f32[16,128,512]{2,1,0:T(8,128)}, f32[2,32,16,512]{3,2,1,0:T(8,128)}, f32[16,32]{1,0:T(8,128)}, f32[1,16]{1,0:T(1,128)}) custom-call(f32[16,128,512]{2,1,0:T(8,128)} %get-tuple-element.12.partial_ref, f32[32,12,128]{2,1,0:T(8,128)} %get-tuple-element.13.spec_ref, f32[32,8,128]{2,1,0:T(8,128)} %get-tuple-element.14.back_ref, ...), custom_call_target="tpu_custom_call" | custom-call | tf_op jit(solution)/shard_map/pallas_call | solution.py:771

commit v3 on v2

--- a/solution.py
+++ b/solution.py
@@ -15,6 +15,7 @@
 MODES = A * M
 RB = 8
 FOLD = 32
+GROUP = 1
 F32 = jnp.float32
 BF16 = jnp.bfloat16
 FULL_TURN = 6.283185307179586
@@ -197,7 +198,7 @@
     rows2_ref, rows3_ref, cols2_ref, wide3_ref, table_sem,
     fbuf, load_sem, wbuf, w_sem, f2_ref, pre_ref, kron2_ref, kronb_ref, tall_ref,
     x1, landed1, send1, gat1, x2, landed2, send2, gat2, rs_send, rs_recv, ag_send, ag_recv,
-    grouped, came, trade_send, trade_recv, pts, ids_ref, vm_ref, hot_ref, cot_ref, half_ref,
+    grouped, came, trade_send, trade_recv, pts, ids_ref, vm_ref, hot_a, hot_b, cot_ref, half_ref,
     sl_ref, other_ref, swap_send, swap_recv, acc_ref, gpx, gpl, gp_send, gp_recv, out_sem,
 ):
     forward_scale, mix_scale = scales
@@ -295,6 +296,13 @@
     backward_point = exact(exact(pick, point_ref[...]), turned)
     kronb_ref[...] = stacked(jnp.where(same, backward_point, 0.0), 0)
     acc_ref[...] = jnp.zeros_like(acc_ref)
+    cells = (cell_ref[...] + 1).astype(F32)
+    vals = jnp.concatenate(
+        (res_ref[...], jnp.broadcast_to(cells, (8, cells.shape[1]))), axis=0
+    )
+    cap = grouped.shape[2]
+    pack(dest_ref[...], vals, grouped, n, cap)
+
     for one in table_loads:
         one.wait()
 
@@ -305,8 +313,6 @@
             hi, low = split2(fbuf[i, :, u * RB : (u + 1) * RB, :].reshape(inputs * RB, width))
             f2_ref[b, : inputs * RB, :] = hi
             f2_ref[b, inputs * RB :, :] = low
-            both = mm(kron2_ref[...], hi)
-            pre_ref[b] = both[:rows] + both[rows:] + mm(kron2_ref[:rows, :], low)
             at = pl.multiple_of(ch * rows, rows)
             mine = jnp.concatenate(
                 (f2_ref[b, pl.ds(at, rows), :], f2_ref[b, pl.ds(at + inputs * RB, rows), :]), axis=0
@@ -387,19 +393,21 @@
 
     scatter_start(x1, landed1, 0, forward_scale)
 
-    cells = (cell_ref[...] + 1).astype(F32)
-    vals = jnp.concatenate(
-        (res_ref[...], jnp.broadcast_to(cells, (8, cells.shape[1]))), axis=0
-    )
-    cap = grouped.shape[2]
-    pack(dest_ref[...], vals, grouped, n, cap)
-
     def trade(k):
         p = rest_of(me + k, n)
         return remote(grouped.at[p], came.at[k], trade_send, trade_recv, p * 2 + ch)
 
     some(1, n, lambda k: trade(k).start())
     came[0] = grouped[me]
+
+    def pointwise(i):
+        for u in range(subs):
+            b = i * subs + u
+            both = mm(kron2_ref[...], f2_ref[b, : inputs * RB, :])
+            low = f2_ref[b, inputs * RB :, :]
+            pre_ref[b] = both[:rows] + both[rows:] + mm(kron2_ref[:rows, :], low)
+
+    each(0, steps, pointwise)
 
     def mix():
         s8 = reduced(x1, landed1, 0)
@@ -453,10 +461,12 @@
     each(0, own, fill)
     span = half_own * FOLD
 
-    def place(q):
+    def name_columns(q, hot_ref):
         for at in range(0, width, 128):
             names = (iota((points, 128), 1) + (q * width + at)).astype(F32)
             hot_ref[:, at : at + 128] = sel(ids_ref[...] == names).astype(BF16)
+
+    def place(q, hot_ref):
         for group in range(2):
             got = mm(vm_ref[group], hot_ref[...])
             got = (got[:span] + got[span:]).reshape(half_own, FOLD, width)
@@ -465,7 +475,14 @@
                 pl.ds(pl.multiple_of(q * FOLD, FOLD), FOLD), :,
             ] = got
 
-    each(0, height // FOLD, place)
+    def place_pair(i):
+        name_columns(2 * i + 1, hot_b)
+        place(2 * i, hot_a)
+        name_columns(2 * i + 2, hot_a)
+        place(2 * i + 1, hot_b)
+
+    name_columns(0, hot_a)
+    each(0, height // FOLD // 2, place_pair)
 
     gather_wait(gat1, 0)
     re = jnp.concatenate((gat1[:, 8, :], gat1[:, 9, :]), axis=1)
@@ -485,8 +502,8 @@
     k0 = math.sqrt(2.0 / math.pi)
 
     def slopes(i):
-        for u in range(subs):
-            b = i * subs + u
+        for u in range(GROUP * subs):
+            b = i * (GROUP * subs) + u
             first = pl.multiple_of(b * RB, RB)
             half = half_ref[:, pl.ds(first, RB), :].reshape(rows, 6 * M).astype(BF16)
             pre = pre_ref[b] + mm(half, wide3_ref[...])
@@ -500,9 +517,10 @@
             sl_ref[b, :rows, :] = hi
             sl_ref[b, rows:, :] = low
             put_tall(tall_ref, first, col_modes(sl_ref[b], cols2_ref[...]), own)
-        swap(i).start()
-
-    each(0, steps, slopes)
+            if u % subs == subs - 1:
+                swap(i * GROUP + u // subs).start()
+
+    each(0, steps // GROUP, slopes)
     scatter_start(x2, landed2, 1, mix_scale)
 
     def point_sums(i):
@@ -648,6 +666,7 @@
             pltpu.VMEM((points, 128), F32),
             pltpu.VMEM((2, own * FOLD, points), BF16),
             pltpu.VMEM((points, width), BF16),
+            pltpu.VMEM((points, width), BF16),
             pltpu.VMEM((own, height, width), F32),
             pltpu.VMEM((own, height, 6 * M), F32),
             pltpu.VMEM((blocks, 2 * rows, width), BF16),
@@ -681,104 +700,119 @@
     scales, partial_ref, spec_ref, back_ref, gp_ref, kept_ref, rows3_hbm, wide3_hbm,
     out_ref, gs_ref, point_ref, bias_ref,
     half_ref, spec_t, grad_t, point_t, rows3_ref, wide3_ref, table_sem,
+    held, load_sem, made, out_sem, gs_sem,
 ):
     grad_scale, norm_points, bias_scale = scales
-    step = pl.program_id(0)
-    own, block, width = out_ref.shape
+    steps, own, block, width = held.shape
     rows = own * RB
-    height = half_ref.shape[1]
-    each = gs_ref.shape[1]
+    height = steps * block
     inputs = 2 * own
-
-    @pl.when(step == 0)
-    def _():
-        row_at = pl.multiple_of(lax.axis_index("row") * height, 128)
-        col_at = pl.multiple_of(lax.axis_index("col") * width, 128)
-        loads = [
-            pltpu.make_async_copy(
-                rows3_hbm.at[pl.ds(row_at, height), :], rows3_ref, table_sem.at[0]
-            ),
-            pltpu.make_async_copy(
-                wide3_hbm.at[:, pl.ds(col_at, width)], wide3_ref, table_sem.at[1]
-            ),
-        ]
-        for one in loads:
-            one.start()
-        kept = as_column(kept_ref[...], lax.axis_index("ch") * own, own)
-        mode = iota((own, MODES), 1)
-        row_mode = mode // M
-        rank = jnp.where(row_mode < M, row_mode, A - 1 - row_mode)
-        keep = jnp.where((rank < kept) & (mode % M < kept), grad_scale, 0.0)
-        biases = jnp.zeros((1, own), F32)
-        for part in range(2):
-            for octet in range(own // 8):
-                j = part * (own // 8) + octet
-                for t in range(A // 8):
-                    lanes = slice(t * 128, (t + 1) * 128)
-                    lines = slice(octet * 8, octet * 8 + 8)
-                    got = turn_blocks(back_ref[t * 8 : t * 8 + 8, 4 + j, :])
-                    if part == 0 and t == 0:
-                        shape = (8, own)
-                        named = iota(shape, 1) == iota(shape, 0) + octet * 8
-                        named = jnp.where(named, got[:, :1] * bias_scale, 0.0)
-                        biases = biases + jnp.sum(named, axis=0, keepdims=True)
-                    grad_t[part, lines, lanes] = got * keep[lines, lanes]
-                    for side in range(2):
-                        at = side * own + octet * 8
-                        spec_t[part, at : at + 8, lanes] = turn_blocks(
-                            spec_ref[t * 8 : t * 8 + 8, side * 4 + j, :]
-                        )
-        bias_ref[...] = biases
-        gp = gp_ref[...] * norm_points
-        into = 128 // own
-        for k in range(into):
-            for i in range(inputs // into):
-                at = i * into + k
-                point_t[at : at + 1, :] = gp[i : i + 1, k * own : (k + 1) * own]
-        eye = sel(iota((own, own), 0) == iota((own, own), 1))
-        point_ref[...] = exact(eye, point_t[...], NT)
-        for one in loads:
-            one.wait()
-        re = jnp.concatenate((back_ref[:, 0, :], back_ref[:, 1, :]), axis=1)
-        im = jnp.concatenate((back_ref[:, 2, :], back_ref[:, 3, :]), axis=1)
-        mode_half(re, im, rows3_ref[...], half_ref)
-
-    for u in range(block // RB):
-        at = slice(u * RB, (u + 1) * RB)
-        first = pl.multiple_of(step * block + u * RB, RB)
-        half = half_ref[:, pl.ds(first, RB), :].reshape(rows, 6 * M).astype(BF16)
-        result = mm(half, wide3_ref[...]).reshape(own, RB, width)
-        out_ref[:, at, :] = partial_ref[:, at, :] + result
-    for i in range(each):
-        c = step * each + i
-        spec_re = spec_t[0, pl.ds(c, 1), :]
-        spec_im = spec_t[1, pl.ds(c, 1), :]
-        gs_ref[0, i] = grad_t[0] * spec_re + grad_t[1] * spec_im
-        gs_ref[1, i] = grad_t[1] * spec_re - grad_t[0] * spec_im
-
-
-def whole(shape):
-    return pl.BlockSpec(shape, lambda i: (0,) * len(shape))
+    each_c = inputs // steps
+
+    def load(i):
+        at = pl.ds(pl.multiple_of(i * block, block), block)
+        return pltpu.make_async_copy(partial_ref.at[:, at, :], held.at[i], load_sem.at[i])
+
+    def store(i):
+        at = pl.ds(pl.multiple_of(i * block, block), block)
+        return pltpu.make_async_copy(held.at[i], out_ref.at[:, at, :], out_sem.at[i])
+
+    def store_gs(i):
+        at = pl.ds(i * each_c, each_c)
+        return pltpu.make_async_copy(made.at[:, at], gs_ref.at[:, at], gs_sem.at[i])
+
+    def each(low, high, body):
+        def go(k, carry):
+            body(k)
+            return carry
+
+        lax.fori_loop(low, high, go, 0)
+
+    row_at = pl.multiple_of(lax.axis_index("row") * height, 128)
+    col_at = pl.multiple_of(lax.axis_index("col") * width, 128)
+    loads = [
+        pltpu.make_async_copy(rows3_hbm.at[pl.ds(row_at, height), :], rows3_ref, table_sem.at[0]),
+        pltpu.make_async_copy(wide3_hbm.at[:, pl.ds(col_at, width)], wide3_ref, table_sem.at[1]),
+    ]
+    for one in loads:
+        one.start()
+    each(0, steps, lambda i: load(i).start())
+    kept = as_column(kept_ref[...], lax.axis_index("ch") * own, own)
+    mode = iota((own, MODES), 1)
+    row_mode = mode // M
+    rank = jnp.where(row_mode < M, row_mode, A - 1 - row_mode)
+    keep = jnp.where((rank < kept) & (mode % M < kept), grad_scale, 0.0)
+    biases = jnp.zeros((1, own), F32)
+    for part in range(2):
+        for octet in range(own // 8):
+            j = part * (own // 8) + octet
+            for t in range(A // 8):
+                lanes = slice(t * 128, (t + 1) * 128)
+                lines = slice(octet * 8, octet * 8 + 8)
+                got = turn_blocks(back_ref[t * 8 : t * 8 + 8, 4 + j, :])
+                if part == 0 and t == 0:
+                    shape = (8, own)
+                    named = iota(shape, 1) == iota(shape, 0) + octet * 8
+                    named = jnp.where(named, got[:, :1] * bias_scale, 0.0)
+                    biases = biases + jnp.sum(named, axis=0, keepdims=True)
+                grad_t[part, lines, lanes] = got * keep[lines, lanes]
+                for side in range(2):
+                    at = side * own + octet * 8
+                    spec_t[part, at : at + 8, lanes] = turn_blocks(
+                        spec_ref[t * 8 : t * 8 + 8, side * 4 + j, :]
+                    )
+
+    def spectral(i):
+        for u in range(each_c):
+            c = i * each_c + u
+            spec_re = spec_t[0, pl.ds(c, 1), :]
+            spec_im = spec_t[1, pl.ds(c, 1), :]
+            made[0, c] = grad_t[0] * spec_re + grad_t[1] * spec_im
+            made[1, c] = grad_t[1] * spec_re - grad_t[0] * spec_im
+        store_gs(i).start()
+
+    each(0, steps, spectral)
+    for one in loads:
+        one.wait()
+    re = jnp.concatenate((back_ref[:, 0, :], back_ref[:, 1, :]), axis=1)
+    im = jnp.concatenate((back_ref[:, 2, :], back_ref[:, 3, :]), axis=1)
+    mode_half(re, im, rows3_ref[...], half_ref)
+
+    def fields(i):
+        load(i).wait()
+        for u in range(block // RB):
+            at = slice(u * RB, (u + 1) * RB)
+            first = pl.multiple_of(i * block + u * RB, RB)
+            half = half_ref[:, pl.ds(first, RB), :].reshape(rows, 6 * M).astype(BF16)
+            result = mm(half, wide3_ref[...]).reshape(own, RB, width)
+            held[i, :, at, :] = held[i, :, at, :] + result
+        store(i).start()
+
+    each(0, steps, fields)
+    bias_ref[...] = biases
+    gp = gp_ref[...] * norm_points
+    into = 128 // own
+    for k in range(into):
+        for i in range(inputs // into):
+            at = i * into + k
+            point_t[at : at + 1, :] = gp[i : i + 1, k * own : (k + 1) * own]
+    eye = sel(iota((own, own), 0) == iota((own, own), 1))
+    point_ref[...] = exact(eye, point_t[...], NT)
+    each(0, steps, lambda i: store(i).wait())
+    each(0, steps, lambda i: store_gs(i).wait())
 
 
 def back_pass(partial, spec, back, gp, kept, rows3, wide3, scales):
     own, height, width = partial.shape
     block = 4 * RB
     steps = height // block
-    each = 2 * own // steps
     hbm = pl.BlockSpec(memory_space=pl.ANY)
-    tile = pl.BlockSpec((own, block, width), lambda i: (0, i, 0))
+    vmem = pl.BlockSpec(memory_space=pltpu.VMEM)
+    dma = pltpu.SemaphoreType.DMA
     return pl.pallas_call(
         functools.partial(back_kernel, scales),
-        grid=(steps,),
-        in_specs=[tile, whole(spec.shape), whole(back.shape), whole(gp.shape), whole(kept.shape)]
-        + [hbm, hbm],
-        out_specs=[
-            tile,
-            pl.BlockSpec((2, each, own, MODES), lambda i: (0, i, 0, 0)),
-            whole((own, 2 * own)),
-            whole((1, own)),
-        ],
+        in_specs=[hbm, vmem, vmem, vmem, vmem, hbm, hbm],
+        out_specs=[hbm, hbm, vmem, vmem],
         out_shape=[
             jax.ShapeDtypeStruct((own, height, width), F32),
             jax.ShapeDtypeStruct((2, 2 * own, own, MODES), F32),
@@ -792,7 +826,12 @@
             pltpu.VMEM((2 * own, own), F32),
             pltpu.VMEM((height, rows3.shape[1]), BF16),
             pltpu.VMEM((wide3.shape[0], width), BF16),
-            pltpu.SemaphoreType.DMA((2,)),
+            dma((2,)),
+            pltpu.VMEM((steps, own, block, width), F32),
+            dma((steps,)),
+            pltpu.VMEM((2, 2 * own, own, MODES), F32),
+            dma((steps,)),
+            dma((steps,)),
         ],
         compiler_params=pltpu.CompilerParams(vmem_limit_bytes=58 * MIB),
     )(partial, spec, back, gp, kept, rows3, wide3)

time: 64.3 us -> 60 us (0.933)
  Pallas kernels: 63.4 us -> 59.1 us
    pallas_call x1, Pallas kernels: 9.01 us -> 6.71 us  [back_pass(): pl.pallas_call(functools.partial(back_kernel, scales), in_specs=[hbm, vme...]
    pallas_call x1, Pallas kernels: 54.4 us -> 52.4 us  [main_pass(): pl.pallas_call(functools.partial(main_kernel, n_row, n_col, scales), out_...]
where the time goes in v3:
time: 60 us; the launch traced here: 59.8 us
  Pallas kernels  59.1 us (98%)
  between operations  0.64 us (1%)
    pallas_call x1, Pallas kernels, main_pass(): pl.pallas_call(functools.partial(main_kernel, n_row, n_col, scales), out_...  52.4 us
    pallas_call x1, Pallas kernels, back_pass(): pl.pallas_call(functools.partial(back_kernel, scales), in_specs=[hbm, vme...  6.71 us

profile of v3, /device:TPU:0, one launch (start us, length us, event | category | flops | bytes accessed | tf_op | source)
XLA Modules:
  0.0 59.8 jit_solution(1350473326949967776)
XLA Ops:
  0.6 52.4 %shard_map.147 = (f32[16,128,512]{2,1,0:T(8,128)}, f32[32,12,128]{2,1,0:T(8,128)}, f32[32,8,128]{2,1,0:T(8,128)}, f32[4,128]{1,0:T(4,128)}) custom-call(s32[1,1024]{1,0:T(1,128)} %bitcast.6, s32[1,1024]{1,0:T(1,128)} %bitcast.7, f32[16,1024]{1,0:T(8,128)} %res_ref.1, s32[1,32]{1,0:T(1,128)} %bitcast.8, f32[1,16]{1,0:T(1,128)} %bitcast.10, ...), custom_call_target="tpu_custom_call" | custom-call | tf_op jit(solution)/shard_map/pallas_call | solution.py:624
  53.1 6.7 %shard_map.148 = (f32[16,128,512]{2,1,0:T(8,128)}, f32[2,32,16,512]{3,2,1,0:T(8,128)}, f32[16,32]{1,0:T(8,128)}, f32[1,16]{1,0:T(1,128)}) custom-call(f32[16,128,512]{2,1,0:T(8,128)} %get-tuple-element.12.partial_ref, f32[32,12,128]{2,1,0:T(8,128)} %get-tuple-element.13.spec_ref, f32[32,8,128]{2,1,0:T(8,128)} %get-tuple-element.14.back_ref, ...), custom_call_target="tpu_custom_call" | custom-call | tf_op jit(solution)/shard_map/pallas_call | solution.py:812

commit v4 on v3

--- a/solution.py
+++ b/solution.py
@@ -15,7 +15,6 @@
 MODES = A * M
 RB = 8
 FOLD = 32
-GROUP = 1
 F32 = jnp.float32
 BF16 = jnp.bfloat16
 FULL_TURN = 6.283185307179586
@@ -47,9 +46,10 @@
     rows2 = np.concatenate((hi, low), axis=0)
     rows3 = np.concatenate((hi.T, low.T, hi.T), axis=1)
     hi, low = np_split(np.concatenate((cos, sin), axis=0))
-    cols2 = np.concatenate((hi.T, low.T), axis=1)
+    gap = np.zeros((n_cols, 128 - 2 * M), ml_dtypes.bfloat16)
+    cols2 = np.concatenate((hi.T, gap, low.T, gap), axis=1)
     hi, low = np_split(np.concatenate((cos, -sin), axis=0))
-    wide3 = np.concatenate((hi, hi, low), axis=0)
+    wide3 = np.concatenate([hi] * 8 + [low] * 4, axis=0)
     return rows2, rows3, cols2, wide3
 
 
@@ -65,11 +65,6 @@
 def stacked(x, axis):
     hi, low = split2(x)
     return jnp.concatenate((hi.astype(F32), low.astype(F32)), axis=axis).astype(BF16)
-
-
-def deep_left(x):
-    hi = x.astype(BF16).astype(F32)
-    return jnp.concatenate((hi, x - hi, hi), axis=1)
 
 
 def deep_right(x):
@@ -113,13 +108,18 @@
             out_ref[(first + at) // cap] = got[:, at : at + cap]
 
 
-def mode_lines(rows2, tall, scale):
-    side = tall.shape[1] // 2
-    both = mm(rows2, stacked(tall, 1))
-    grid = both[: 2 * A, : 2 * side] + both[2 * A :, : 2 * side] + both[: 2 * A, 2 * side :]
-    re = (grid[:A, :side] - grid[A:, side:]) * scale
-    im = (grid[A:, :side] + grid[:A, side:]) * (-scale)
-    return [part[:, at : at + 128] for part in (re, im) for at in range(0, side, 128)]
+def mode_lines(rows2, tall_ref, x_ref, scale):
+    height = tall_ref.shape[0] * RB
+    for o in range(tall_ref.shape[1] // RB):
+        tall = tall_ref[:, o * RB : (o + 1) * RB, :].reshape(height, 2 * M)
+        hi, low = split2(tall)
+        both = mm(rows2, hi)
+        grid = both[: 2 * A] + both[2 * A :] + mm(rows2[: 2 * A], low)
+        re = (grid[:A, :M] - grid[A:, M:]) * scale
+        im = (grid[A:, :M] + grid[:A, M:]) * (-scale)
+        octet, at = o // 8, o % 8 * M
+        x_ref[:, octet, at : at + M] = re
+        x_ref[:, 2 + octet, at : at + M] = im
 
 
 def part_of(x, size):
@@ -155,39 +155,37 @@
 
 
 def compact8(re, im, a):
-    y = jnp.concatenate((re, im), axis=0)
-    group = iota(y.shape, 1) // M
-    y = jnp.where(group == lax.rem(a, 8), y, 0.0)
-    y = exact(y, same_place())
-    y = jnp.where(group == iota(y.shape, 0) % 8, y, 0.0)
-    return jnp.sum(y.reshape(8, 8, 128), axis=1)
-
-
-def mode_half(re, im, rows3, half_ref):
-    grid = jnp.concatenate(
-        (jnp.concatenate((re, im), axis=1), jnp.concatenate((-im, re), axis=1)), axis=0
-    )
-    half = mm(rows3, deep_right(grid))
-    side = half.shape[1] // 2
-    for o in range(side // M):
-        at = o * M
-        pair = jnp.concatenate((half[:, at : at + M], half[:, side + at : side + at + M]), axis=1)
-        half_ref[o] = deep_left(pair)
-
-
-def put_tall(tall_ref, first, tall, own):
-    for c in range(own):
-        for part in range(2):
-            at = (part * own + c) * M
-            tall_ref[pl.ds(first, RB), at : at + M] = tall[
-                c * RB : (c + 1) * RB, part * M : (part + 1) * M
-            ]
+    group = iota(re.shape, 1) // M
+    mine = group == rest_of(a, 8)
+    pair = jnp.concatenate((jnp.where(mine, re, 0.0), jnp.where(mine, im, 0.0)), axis=0)
+    pair = exact(pair, same_place())
+    count = re.shape[0]
+    want = iota(re.shape, 0) % 4 * 2
+    y = jnp.where(group == want, pair[:count], jnp.where(group == want + 1, pair[count:], 0.0))
+    fours = sel(iota((8, count), 0) == iota((8, count), 1) // 4)
+    return exact(fours, y)
+
+
+def mode_half(lines, rows3, half_ref):
+    for q, x in enumerate(lines):
+        lane = iota(x.shape, 1)
+        low_half = lane % (2 * M) < M
+        y = jnp.where(low_half, -pltpu.roll(x, 128 - M, 1), pltpu.roll(x, M, 1))
+        half = mm(rows3, deep_right(jnp.concatenate((x, y), axis=0)))
+        own = iota(half.shape, 1) // (2 * M)
+        for k in range(4):
+            half_ref[q * 4 + k] = jnp.where(own == k, half, 0.0)
+
+
+def from_half(half, wide3):
+    hi, low = split2(half)
+    return mm(jnp.concatenate((hi, low), axis=1), wide3[:256]) + mm(hi, wide3[256:])
 
 
 def col_modes(parts, cols2):
     half = parts.shape[0] // 2
     got = mm(parts, cols2)
-    return got[:half, : 2 * M] + got[:half, 2 * M :] + got[half:, : 2 * M]
+    return got[:half, : 2 * M] + got[:half, 128 : 128 + 2 * M] + got[half:, : 2 * M]
 
 
 def main_kernel(
@@ -302,6 +300,15 @@
     )
     cap = grouped.shape[2]
     pack(dest_ref[...], vals, grouped, n, cap)
+    pl.semaphore_wait(barrier, count - 1)
+
+    def trade(k):
+        p = rest_of(me + k, n)
+        return remote(grouped.at[p], came.at[k], trade_send, trade_recv, p * 2 + ch)
+
+    some(1, n, lambda k: trade(k).start())
+    came[0] = grouped[me]
+
 
     for one in table_loads:
         one.wait()
@@ -313,13 +320,23 @@
             hi, low = split2(fbuf[i, :, u * RB : (u + 1) * RB, :].reshape(inputs * RB, width))
             f2_ref[b, : inputs * RB, :] = hi
             f2_ref[b, inputs * RB :, :] = low
-            at = pl.multiple_of(ch * rows, rows)
+
+    def front_modes(i):
+        at = pl.multiple_of(ch * rows, rows)
+        for u in range(subs):
+            b = i * subs + u
             mine = jnp.concatenate(
                 (f2_ref[b, pl.ds(at, rows), :], f2_ref[b, pl.ds(at + inputs * RB, rows), :]), axis=0
             )
-            put_tall(tall_ref, pl.multiple_of(b * RB, RB), col_modes(mine, cols2_ref[...]), own)
-
-    each(0, steps, front)
+            tall_ref[b] = col_modes(mine, cols2_ref[...])
+
+    def front_next(i):
+        front(i)
+        front_modes(i - 1)
+
+    front(0)
+    each(1, steps, front_next)
+    front_modes(steps - 1)
 
     def scatter(x, landed, stage):
         def copy(k):
@@ -333,12 +350,8 @@
         return copy
 
     def scatter_start(x, landed, stage, scale):
-        lines = mode_lines(rows2_ref[...], tall_ref[...], scale)
-        for j, line in enumerate(lines):
-            x[:, j, :] = line
+        mode_lines(rows2_ref[...], tall_ref, x, scale)
         copy = scatter(x, landed, stage)
-        if stage == 0:
-            pl.semaphore_wait(barrier, count - 1)
         some(1, A, lambda k: copy(k).start())
         off_reducer(lambda: copy(0).start())
 
@@ -393,13 +406,6 @@
 
     scatter_start(x1, landed1, 0, forward_scale)
 
-    def trade(k):
-        p = rest_of(me + k, n)
-        return remote(grouped.at[p], came.at[k], trade_send, trade_recv, p * 2 + ch)
-
-    some(1, n, lambda k: trade(k).start())
-    came[0] = grouped[me]
-
     def pointwise(i):
         for u in range(subs):
             b = i * subs + u
@@ -408,6 +414,42 @@
             pre_ref[b] = both[:rows] + both[rows:] + mm(kron2_ref[:rows, :], low)
 
     each(0, steps, pointwise)
+
+    came_all = came.at[pl.ds(1, n - 1)]
+    remote(came_all, came_all, trade_send, trade_recv, flat).wait_recv()
+    for p in range(n):
+        pts[:, p * cap : (p + 1) * cap] = came[p]
+    cell = pts[own : own + 1, :].astype(jnp.int32) - 1
+    row = cell // width
+    fold = jnp.where(cell < 0, -1, row % FOLD)
+    code = jnp.where(cell < 0, -1, row // FOLD * width + cell % width).astype(F32)
+    for first in range(0, points, 128):
+        ids_ref[first : first + 128, :] = jnp.broadcast_to(
+            code[:, first : first + 128], (128, 128)
+        ).T
+    here = fold == iota((FOLD, points), 0)
+    half_own = own // 2
+
+    def fill(o):
+        value = pts[pl.ds(o, 1), :]
+        hi = value.astype(BF16).astype(F32)
+        group = o // half_own
+        at = pl.multiple_of(lax.rem(o, half_own) * FOLD, FOLD)
+        vm_ref[group, pl.ds(at, FOLD), :] = jnp.where(here, hi, 0.0).astype(BF16)
+        vm_ref[group, pl.ds(at + half_own * FOLD, FOLD), :] = jnp.where(
+            here, value - hi, 0.0
+        ).astype(BF16)
+
+    each(0, own, fill)
+
+    span = half_own * FOLD
+
+    def name_columns(q, hot_ref):
+        for at in range(0, width, 128):
+            names = (iota((points, 128), 1) + (q * width + at)).astype(F32)
+            hot_ref[:, at : at + 128] = sel(ids_ref[...] == names).astype(BF16)
+
+    name_columns(0, hot_a)
 
     def mix():
         s8 = reduced(x1, landed1, 0)
@@ -423,8 +465,7 @@
         mixed = compact8(re * keep, im * keep, a)
         for d in range(2):
             send1[d, :8] = s8
-            send1[d, 8:10] = mixed[2 * d : 2 * d + 2]
-            send1[d, 10:12] = mixed[4 + 2 * d : 6 + 2 * d]
+            send1[d, 8:12] = mixed[4 * d : 4 * d + 4]
         copy = gather(send1, gat1, 0)
         some(1, count, lambda k: copy(k).start())
         gat1[a] = send1[ch]
@@ -432,39 +473,6 @@
     on_reducer(mix)
     if stride > 1:
         off_reducer(lambda: w_load.wait())
-
-    came_all = came.at[pl.ds(1, n - 1)]
-    remote(came_all, came_all, trade_send, trade_recv, flat).wait_recv()
-    for p in range(n):
-        pts[:, p * cap : (p + 1) * cap] = came[p]
-    cell = pts[own : own + 1, :].astype(jnp.int32) - 1
-    row = cell // width
-    fold = jnp.where(cell < 0, -1, row % FOLD)
-    code = jnp.where(cell < 0, -1, row // FOLD * width + cell % width).astype(F32)
-    for first in range(0, points, 128):
-        ids_ref[first : first + 128, :] = jnp.broadcast_to(
-            code[:, first : first + 128], (128, 128)
-        ).T
-    here = fold == iota((FOLD, points), 0)
-    half_own = own // 2
-
-    def fill(o):
-        value = pts[pl.ds(o, 1), :]
-        hi = value.astype(BF16).astype(F32)
-        group = o // half_own
-        at = pl.multiple_of(lax.rem(o, half_own) * FOLD, FOLD)
-        vm_ref[group, pl.ds(at, FOLD), :] = jnp.where(here, hi, 0.0).astype(BF16)
-        vm_ref[group, pl.ds(at + half_own * FOLD, FOLD), :] = jnp.where(
-            here, value - hi, 0.0
-        ).astype(BF16)
-
-    each(0, own, fill)
-    span = half_own * FOLD
-
-    def name_columns(q, hot_ref):
-        for at in range(0, width, 128):
-            names = (iota((points, 128), 1) + (q * width + at)).astype(F32)
-            hot_ref[:, at : at + 128] = sel(ids_ref[...] == names).astype(BF16)
 
     def place(q, hot_ref):
         for group in range(2):
@@ -481,17 +489,21 @@
         name_columns(2 * i + 2, hot_a)
         place(2 * i + 1, hot_b)
 
-    name_columns(0, hot_a)
     each(0, height // FOLD // 2, place_pair)
 
     gather_wait(gat1, 0)
-    re = jnp.concatenate((gat1[:, 8, :], gat1[:, 9, :]), axis=1)
-    im = jnp.concatenate((gat1[:, 10, :], gat1[:, 11, :]), axis=1)
-    bias_shape = (own, own * M)
-    bias_at = sel(iota(bias_shape, 1) == iota(bias_shape, 0) * M)
+    bias_shape = (own, own * 2 * M)
+    bias_at = sel(iota(bias_shape, 1) == iota(bias_shape, 0) * (2 * M))
     bias_line = exact(jnp.broadcast_to(bias_ref[...], (8, own)), bias_at)[:1]
-    re = re + jnp.where(iota(re.shape, 0) == 0, bias_line, 0.0)
-    mode_half(re, im, rows3_ref[...], half_ref)
+    first_mode = iota((A, 128), 0) == 0
+    mode_half(
+        [
+            gat1[:, 8 + q, :]
+            + jnp.where(first_mode, bias_line[:, q * 128 : (q + 1) * 128], 0.0)
+            for q in range(4)
+        ],
+        rows3_ref[...], half_ref,
+    )
 
     def swap(i):
         at = pl.ds(i * subs, subs)
@@ -502,11 +514,11 @@
     k0 = math.sqrt(2.0 / math.pi)
 
     def slopes(i):
-        for u in range(GROUP * subs):
-            b = i * (GROUP * subs) + u
+        for u in range(subs):
+            b = i * subs + u
             first = pl.multiple_of(b * RB, RB)
-            half = half_ref[:, pl.ds(first, RB), :].reshape(rows, 6 * M).astype(BF16)
-            pre = pre_ref[b] + mm(half, wide3_ref[...])
+            half = half_ref[:, pl.ds(first, RB), :].reshape(rows, 128)
+            pre = pre_ref[b] + from_half(half, wide3_ref)
             cot = cot_ref[:, pl.ds(first, RB), :].reshape(rows, width)
             square = pre * pre
             t = jnp.tanh(k0 * pre * (1.0 + 0.044715 * square))
@@ -516,11 +528,21 @@
             hi, low = split2(slope)
             sl_ref[b, :rows, :] = hi
             sl_ref[b, rows:, :] = low
-            put_tall(tall_ref, first, col_modes(sl_ref[b], cols2_ref[...]), own)
             if u % subs == subs - 1:
-                swap(i * GROUP + u // subs).start()
-
-    each(0, steps // GROUP, slopes)
+                swap(i).start()
+
+    def slope_modes(i):
+        for u in range(subs):
+            b = i * subs + u
+            tall_ref[b] = col_modes(sl_ref[b], cols2_ref[...])
+
+    def slopes_next(i):
+        slope_modes(i - 1)
+        slopes(i)
+
+    slopes(0)
+    each(1, steps, slopes_next)
+    slope_modes(steps - 1)
     scatter_start(x2, landed2, 1, mix_scale)
 
     def point_sums(i):
@@ -559,8 +581,7 @@
         im = jnp.concatenate(lines_im, axis=0) * forward_scale
         turned_modes = compact8(re, im, a)
         for d in range(2):
-            send2[d, :2] = turned_modes[2 * d : 2 * d + 2]
-            send2[d, 2:4] = turned_modes[4 + 2 * d : 6 + 2 * d]
+            send2[d, :4] = turned_modes[4 * d : 4 * d + 4]
             send2[d, 4:8] = s8[4 * d : 4 * d + 4]
         copy = gather(send2, gat2, 1)
         some(1, count, lambda k: copy(k).start())
@@ -645,7 +666,7 @@
             pltpu.VMEM((blocks, rows, width), F32),
             pltpu.VMEM((2 * rows, inputs * RB), BF16),
             pltpu.VMEM((2 * rows, inputs * RB), BF16),
-            pltpu.VMEM((height, 2 * own * M), F32),
+            pltpu.VMEM((blocks, rows, 2 * M), F32),
             pltpu.VMEM((A, 4, 128), F32),
             pltpu.VMEM((count, 4, 128), F32),
             pltpu.VMEM((2, 12, 128), F32),
@@ -668,7 +689,7 @@
             pltpu.VMEM((points, width), BF16),
             pltpu.VMEM((points, width), BF16),
             pltpu.VMEM((own, height, width), F32),
-            pltpu.VMEM((own, height, 6 * M), F32),
+            pltpu.VMEM((own, height, 128), F32),
             pltpu.VMEM((blocks, 2 * rows, width), BF16),
             pltpu.VMEM((blocks, rows, width), F32),
             dma,
@@ -774,17 +795,15 @@
     each(0, steps, spectral)
     for one in loads:
         one.wait()
-    re = jnp.concatenate((back_ref[:, 0, :], back_ref[:, 1, :]), axis=1)
-    im = jnp.concatenate((back_ref[:, 2, :], back_ref[:, 3, :]), axis=1)
-    mode_half(re, im, rows3_ref[...], half_ref)
+    mode_half([back_ref[:, q, :] for q in range(4)], rows3_ref[...], half_ref)
 
     def fields(i):
         load(i).wait()
         for u in range(block // RB):
             at = slice(u * RB, (u + 1) * RB)
             first = pl.multiple_of(i * block + u * RB, RB)
-            half = half_ref[:, pl.ds(first, RB), :].reshape(rows, 6 * M).astype(BF16)
-            result = mm(half, wide3_ref[...]).reshape(own, RB, width)
+            half = half_ref[:, pl.ds(first, RB), :].reshape(rows, 128)
+            result = from_half(half, wide3_ref).reshape(own, RB, width)
             held[i, :, at, :] = held[i, :, at, :] + result
         store(i).start()
 
@@ -820,7 +839,7 @@
             jax.ShapeDtypeStruct((1, own), F32),
         ],
         scratch_shapes=[
-            pltpu.VMEM((own, height, 6 * M), F32),
+            pltpu.VMEM((own, height, 128), F32),
             pltpu.VMEM((2, 2 * own, MODES), F32),
             pltpu.VMEM((2, own, MODES), F32),
             pltpu.VMEM((2 * own, own), F32),

time: 60 us -> 56.4 us (0.940)
  Pallas kernels: 59.1 us -> 55.4 us
    pallas_call x1, Pallas kernels: 52.4 us -> 48.8 us  [main_pass(): pl.pallas_call(functools.partial(main_kernel, n_row, n_col, scales), out_...]
where the time goes in v4:
time: 56.4 us; the launch traced here: 56.2 us
  Pallas kernels  55.4 us (98%)
  between operations  0.8 us (1%)
    pallas_call x1, Pallas kernels, main_pass(): pl.pallas_call(functools.partial(main_kernel, n_row, n_col, scales), out_...  48.8 us
    pallas_call x1, Pallas kernels, back_pass(): pl.pallas_call(functools.partial(back_kernel, scales), in_specs=[hbm, vme...  6.61 us

profile of v4, /device:TPU:0, one launch (start us, length us, event | category | flops | bytes accessed | tf_op | source)
XLA Modules:
  0.0 56.2 jit_solution(9484501726782498170)
XLA Ops:
  0.6 48.8 %shard_map.147 = (f32[16,128,512]{2,1,0:T(8,128)}, f32[32,12,128]{2,1,0:T(8,128)}, f32[32,8,128]{2,1,0:T(8,128)}, f32[4,128]{1,0:T(4,128)}) custom-call(s32[1,1024]{1,0:T(1,128)} %bitcast.6, s32[1,1024]{1,0:T(1,128)} %bitcast.7, f32[16,1024]{1,0:T(8,128)} %res_ref.1, s32[1,32]{1,0:T(1,128)} %bitcast.8, f32[1,16]{1,0:T(1,128)} %bitcast.10, ...), custom_call_target="tpu_custom_call" | custom-call | tf_op jit(solution)/shard_map/pallas_call | solution.py:645
  49.5 6.6 %shard_map.148 = (f32[16,128,512]{2,1,0:T(8,128)}, f32[2,32,16,512]{3,2,1,0:T(8,128)}, f32[16,32]{1,0:T(8,128)}, f32[1,16]{1,0:T(1,128)}) custom-call(f32[16,128,512]{2,1,0:T(8,128)} %get-tuple-element.12.partial_ref, f32[32,12,128]{2,1,0:T(8,128)} %get-tuple-element.13.spec_ref, f32[32,8,128]{2,1,0:T(8,128)} %get-tuple-element.14.back_ref, ...), custom_call_target="tpu_custom_call" | custom-call | tf_op jit(solution)/shard_map/pallas_call | solution.py:831

commit v5 on v4

--- a/solution.py
+++ b/solution.py
@@ -241,6 +241,15 @@
 
         lax.fori_loop(low, high, go, 0)
 
+    def pairs(low, high, body):
+        def both(i):
+            body(low + 2 * i)
+            body(low + 2 * i + 1)
+
+        each(0, (high - low) // 2, both)
+        if (high - low) % 2:
+            body(high - 1)
+
     def on_reducer(body):
         if stride == 1:
             body()
@@ -335,7 +344,7 @@
         front_modes(i - 1)
 
     front(0)
-    each(1, steps, front_next)
+    pairs(1, steps, front_next)
     front_modes(steps - 1)
 
     def scatter(x, landed, stage):
@@ -413,7 +422,7 @@
             low = f2_ref[b, inputs * RB :, :]
             pre_ref[b] = both[:rows] + both[rows:] + mm(kron2_ref[:rows, :], low)
 
-    each(0, steps, pointwise)
+    pairs(0, steps, pointwise)
 
     came_all = came.at[pl.ds(1, n - 1)]
     remote(came_all, came_all, trade_send, trade_recv, flat).wait_recv()
@@ -541,7 +550,7 @@
         slopes(i)
 
     slopes(0)
-    each(1, steps, slopes_next)
+    pairs(1, steps, slopes_next)
     slope_modes(steps - 1)
     scatter_start(x2, landed2, 1, mix_scale)
 
@@ -606,7 +615,7 @@
             cot_ref[:, pl.ds(first, RB), :] = result.reshape(own, RB, width)
         store(i).start()
 
-    each(0, steps, backs)
+    pairs(0, steps, backs)
 
     gp_all = gpl.at[pl.ds(1, n - 1)]
     remote(gp_all, gp_all, gp_send, gp_recv, flat).wait_recv()
@@ -758,6 +767,21 @@
     for one in loads:
         one.start()
     each(0, steps, lambda i: load(i).start())
+    for one in loads:
+        one.wait()
+    mode_half([back_ref[:, q, :] for q in range(4)], rows3_ref[...], half_ref)
+
+    def fields(i):
+        load(i).wait()
+        for u in range(block // RB):
+            at = slice(u * RB, (u + 1) * RB)
+            first = pl.multiple_of(i * block + u * RB, RB)
+            half = half_ref[:, pl.ds(first, RB), :].reshape(rows, 128)
+            result = from_half(half, wide3_ref).reshape(own, RB, width)
+            held[i, :, at, :] = held[i, :, at, :] + result
+        store(i).start()
+
+    each(0, steps, fields)
     kept = as_column(kept_ref[...], lax.axis_index("ch") * own, own)
     mode = iota((own, MODES), 1)
     row_mode = mode // M
@@ -793,21 +817,6 @@
         store_gs(i).start()
 
     each(0, steps, spectral)
-    for one in loads:
-        one.wait()
-    mode_half([back_ref[:, q, :] for q in range(4)], rows3_ref[...], half_ref)
-
-    def fields(i):
-        load(i).wait()
-        for u in range(block // RB):
-            at = slice(u * RB, (u + 1) * RB)
-            first = pl.multiple_of(i * block + u * RB, RB)
-            half = half_ref[:, pl.ds(first, RB), :].reshape(rows, 128)
-            result = from_half(half, wide3_ref).reshape(own, RB, width)
-            held[i, :, at, :] = held[i, :, at, :] + result
-        store(i).start()
-
-    each(0, steps, fields)
     bias_ref[...] = biases
     gp = gp_ref[...] * norm_points
     into = 128 // own

time: 56.4 us -> 55 us (0.975)
  Pallas kernels: 55.4 us -> 54 us
    pallas_call x1, Pallas kernels: 48.8 us -> 47.3 us  [main_pass(): pl.pallas_call(functools.partial(main_kernel, n_row, n_col, scales), out_...]
where the time goes in v5:
time: 55 us; the launch traced here: 54.8 us
  Pallas kernels  54 us (98%)
  between operations  0.8 us (1%)
    pallas_call x1, Pallas kernels, main_pass(): pl.pallas_call(functools.partial(main_kernel, n_row, n_col, scales), out_...  47.3 us
    pallas_call x1, Pallas kernels, back_pass(): pl.pallas_call(functools.partial(back_kernel, scales), in_specs=[hbm, vme...  6.67 us

profile of v5, /device:TPU:0, one launch (start us, length us, event | category | flops | bytes accessed | tf_op | source)
XLA Modules:
  0.0 54.8 jit_solution(324112370433755371)
XLA Ops:
  0.6 47.3 %shard_map.147 = (f32[16,128,512]{2,1,0:T(8,128)}, f32[32,12,128]{2,1,0:T(8,128)}, f32[32,8,128]{2,1,0:T(8,128)}, f32[4,128]{1,0:T(4,128)}) custom-call(s32[1,1024]{1,0:T(1,128)} %bitcast.6, s32[1,1024]{1,0:T(1,128)} %bitcast.7, f32[16,1024]{1,0:T(8,128)} %res_ref.1, s32[1,32]{1,0:T(1,128)} %bitcast.8, f32[1,16]{1,0:T(1,128)} %bitcast.10, ...), custom_call_target="tpu_custom_call" | custom-call | tf_op jit(solution)/shard_map/pallas_call | solution.py:654
  47.9 6.7 %shard_map.148 = (f32[16,128,512]{2,1,0:T(8,128)}, f32[2,32,16,512]{3,2,1,0:T(8,128)}, f32[16,32]{1,0:T(8,128)}, f32[1,16]{1,0:T(1,128)}) custom-call(f32[16,128,512]{2,1,0:T(8,128)} %get-tuple-element.12.partial_ref, f32[32,12,128]{2,1,0:T(8,128)} %get-tuple-element.13.spec_ref, f32[32,8,128]{2,1,0:T(8,128)} %get-tuple-element.14.back_ref, ...), custom_call_target="tpu_custom_call" | custom-call | tf_op jit(solution)/shard_map/pallas_call | solution.py:840

commit v6 on v5

--- a/solution.py
+++ b/solution.py
@@ -344,7 +344,8 @@
         front_modes(i - 1)
 
     front(0)
-    pairs(1, steps, front_next)
+    for i in range(1, steps):
+        front_next(i)
     front_modes(steps - 1)
 
     def scatter(x, landed, stage):
@@ -422,7 +423,8 @@
             low = f2_ref[b, inputs * RB :, :]
             pre_ref[b] = both[:rows] + both[rows:] + mm(kron2_ref[:rows, :], low)
 
-    pairs(0, steps, pointwise)
+    for i in range(steps):
+        pointwise(i)
 
     came_all = came.at[pl.ds(1, n - 1)]
     remote(came_all, came_all, trade_send, trade_recv, flat).wait_recv()

time: 55 us -> 54.3 us (0.987)
  Pallas kernels: 54 us -> 53.3 us
    pallas_call x1, Pallas kernels: 47.3 us -> 46.6 us  [main_pass(): pl.pallas_call(functools.partial(main_kernel, n_row, n_col, scales), out_...]
where the time goes in v6:
time: 54.3 us; the launch traced here: 54.1 us
  Pallas kernels  53.3 us (98%)
  between operations  0.8 us (1%)
    pallas_call x1, Pallas kernels, main_pass(): pl.pallas_call(functools.partial(main_kernel, n_row, n_col, scales), out_...  46.6 us
    pallas_call x1, Pallas kernels, back_pass(): pl.pallas_call(functools.partial(back_kernel, scales), in_specs=[hbm, vme...  6.67 us

profile of v6, /device:TPU:0, one launch (start us, length us, event | category | flops | bytes accessed | tf_op | source)
XLA Modules:
  0.0 54.1 jit_solution(18245793945011523212)
XLA Ops:
  0.6 46.6 %shard_map.147 = (f32[16,128,512]{2,1,0:T(8,128)}, f32[32,12,128]{2,1,0:T(8,128)}, f32[32,8,128]{2,1,0:T(8,128)}, f32[4,128]{1,0:T(4,128)}) custom-call(s32[1,1024]{1,0:T(1,128)} %bitcast.6, s32[1,1024]{1,0:T(1,128)} %bitcast.7, f32[16,1024]{1,0:T(8,128)} %res_ref.1, s32[1,32]{1,0:T(1,128)} %bitcast.8, f32[1,16]{1,0:T(1,128)} %bitcast.10, ...), custom_call_target="tpu_custom_call" | custom-call | tf_op jit(solution)/shard_map/pallas_call | solution.py:656
  47.3 6.7 %shard_map.148 = (f32[16,128,512]{2,1,0:T(8,128)}, f32[2,32,16,512]{3,2,1,0:T(8,128)}, f32[16,32]{1,0:T(8,128)}, f32[1,16]{1,0:T(1,128)}) custom-call(f32[16,128,512]{2,1,0:T(8,128)} %get-tuple-element.12.partial_ref, f32[32,12,128]{2,1,0:T(8,128)} %get-tuple-element.13.spec_ref, f32[32,8,128]{2,1,0:T(8,128)} %get-tuple-element.14.back_ref, ...), custom_call_target="tpu_custom_call" | custom-call | tf_op jit(solution)/shard_map/pallas_call | solution.py:842
